TPU v7x, 32 devices: a whole 2x2x4 slice. The times are simulated.
32 devices in a mesh: stream: 16 (over z, y, core), batch: 2 (over x).
Axes of the slice: x: 2, y: 2, z: 4, core: 2. Of those that a mesh axis runs over, the one named last changes fastest.
Arguments:
- images: bfloat16 [576, 13, 13, 512], P(('stream', 'batch')), may hold values from -6 to 6
- conv4_weight: bfloat16 [4608, 1024], P('stream'), may hold values from -0.09375 to 0.09375
- conv4_bias: bfloat16 [1024], P('stream'), may hold values from -3 to 3
- conv5_weight: bfloat16 [4608, 1024], P('stream'), may hold values from -0.09375 to 0.09375
- conv5_bias: bfloat16 [1024], P('stream'), may hold values from -3 to 3
- cotangent: bfloat16 [576, 13, 13, 512], P(('stream', 'batch')), may hold values from -6 to 6
Outputs:
- conv5_out: bfloat16 [576, 13, 13, 512], P(('stream', 'batch'))
- images_grad: bfloat16 [576, 13, 13, 512], P(('stream', 'batch'))
- conv4_weight_grad: float32 [4608, 1024], P('stream')
- conv4_bias_grad: float32 [1024], P('stream')
- conv5_weight_grad: float32 [4608, 1024], P('stream')
- conv5_bias_grad: float32 [1024], P('stream')
All inputs are finite; a program needn't handle non-finite values.
Results may differ from a plain program's by a relative error of at most 0.0095.
Values may be sent and summed in bfloat16 or wider, within the bound.
A program may use at most 320 MiB of HBM per device.

v0:
```python
import jax
import jax.numpy as jnp
from jax import lax
from jax.sharding import PartitionSpec as P

CH = 512
SIDE = 13
MICRO = 3


def patch_rows(field):
    image_count = field.shape[0]
    padded = jnp.pad(field, ((0, 0), (1, 1), (1, 1), (0, 0)))
    tap_list = [
        padded[:, row_off : row_off + SIDE, col_off : col_off + SIDE, :]
        for row_off in range(3)
        for col_off in range(3)
    ]
    return jnp.stack(tap_list, 3).reshape(image_count * SIDE * SIDE, 9 * CH)


def fold_rows(grad_rows, image_count):
    pieces = grad_rows.reshape(image_count, SIDE, SIDE, 9, CH)
    padded = jnp.zeros((image_count, SIDE + 2, SIDE + 2, CH), jnp.float32)
    for tap_index in range(9):
        row_off = tap_index // 3
        col_off = tap_index % 3
        padded = padded.at[:, row_off : row_off + SIDE, col_off : col_off + SIDE, :].add(
            pieces[:, :, :, tap_index, :]
        )
    return padded[:, 1 : 1 + SIDE, 1 : 1 + SIDE, :]


def outer_sum(left, right):
    return lax.dot_general(
        left, right, (((0,), (0,)), ((), ())), preferred_element_type=jnp.float32
    )


def back_rows(grad_rows, weight):
    return lax.dot_general(
        grad_rows, weight, (((1,), (1,)), ((), ())), preferred_element_type=jnp.float32
    )


def gelu_slope(pre_act, upstream):
    return jax.vjp(jax.nn.gelu, pre_act)[1](upstream)[0]


def shards(images, conv4_weight, conv4_bias, conv5_weight, conv5_bias, cotangent):
    half_size = lax.axis_size("stream") // 2
    group_id = lax.axis_index("stream") // half_size
    rows_full = 9 * CH
    per_micro = images.shape[0] // MICRO
    acc_weight_four = jnp.zeros((rows_full, CH), jnp.float32)
    acc_bias_four = jnp.zeros((CH,), jnp.float32)
    acc_weight_five = jnp.zeros((rows_full, CH), jnp.float32)
    acc_bias_five = jnp.zeros((CH,), jnp.float32)
    out_list = []
    grad_list = []
    for micro_step in range(MICRO):
        current = (
            lax.dynamic_slice_in_dim(
                lax.all_gather(conv4_weight, "stream", axis=0, tiled=True), group_id * CH, CH, 1
            ),
            lax.dynamic_slice_in_dim(
                lax.all_gather(conv4_bias, "stream", axis=0, tiled=True), group_id * CH, CH, 0
            ).astype(jnp.float32),
            lax.dynamic_slice_in_dim(
                lax.all_gather(conv5_weight, "stream", axis=0, tiled=True), group_id * CH, CH, 1
            ),
            lax.dynamic_slice_in_dim(
                lax.all_gather(conv5_bias, "stream", axis=0, tiled=True), group_id * CH, CH, 0
            ).astype(jnp.float32),
        )
        kernel_four, shift_four, kernel_five, shift_five = current
        field = images[micro_step * per_micro : (micro_step + 1) * per_micro]
        upstream = cotangent[micro_step * per_micro : (micro_step + 1) * per_micro].astype(
            jnp.float32
        )
        upstream = upstream.reshape(per_micro * SIDE * SIDE, CH)
        input_patches = patch_rows(field)
        pre_four = (
            jnp.dot(input_patches, kernel_four, preferred_element_type=jnp.float32) + shift_four
        )
        hidden = jax.nn.gelu(pre_four).astype(jnp.bfloat16)
        hidden_patches = patch_rows(hidden.reshape(per_micro, SIDE, SIDE, CH))
        pre_five = (
            jnp.dot(hidden_patches, kernel_five, preferred_element_type=jnp.float32) + shift_five
        )
        out_list.append(
            jax.nn.gelu(pre_five).astype(jnp.bfloat16).reshape(per_micro, SIDE, SIDE, CH)
        )
        grad_five = gelu_slope(pre_five, upstream).astype(jnp.bfloat16)
        acc_weight_five = acc_weight_five + outer_sum(hidden_patches, grad_five)
        acc_bias_five = acc_bias_five + jnp.sum(grad_five.astype(jnp.float32), axis=0)
        grad_hidden = fold_rows(back_rows(grad_five, kernel_five), per_micro).reshape(
            per_micro * SIDE * SIDE, CH
        )
        grad_four = gelu_slope(pre_four, grad_hidden).astype(jnp.bfloat16)
        acc_weight_four = acc_weight_four + outer_sum(input_patches, grad_four)
        acc_bias_four = acc_bias_four + jnp.sum(grad_four.astype(jnp.float32), axis=0)
        grad_list.append(
            fold_rows(back_rows(grad_four, kernel_four), per_micro).astype(jnp.bfloat16)
        )

    def widen(local_grad, along):
        blank = jnp.zeros_like(local_grad)
        return jnp.where(
            group_id == 0,
            jnp.concatenate([local_grad, blank], along),
            jnp.concatenate([blank, local_grad], along),
        )

    summed = (
        lax.psum_scatter(widen(acc_weight_four, 1), "stream", scatter_dimension=0, tiled=True),
        lax.psum_scatter(widen(acc_bias_four, 0), "stream", scatter_dimension=0, tiled=True),
        lax.psum_scatter(widen(acc_weight_five, 1), "stream", scatter_dimension=0, tiled=True),
        lax.psum_scatter(widen(acc_bias_five, 0), "stream", scatter_dimension=0, tiled=True),
    )
    totals = (
        lax.psum(summed[0].astype(jnp.bfloat16), "batch").astype(jnp.float32),
        lax.psum(summed[1].astype(jnp.bfloat16), "batch").astype(jnp.float32),
        lax.psum(summed[2].astype(jnp.bfloat16), "batch").astype(jnp.float32),
        lax.psum(summed[3].astype(jnp.bfloat16), "batch").astype(jnp.float32),
    )
    return (
        jnp.concatenate(out_list, 0),
        jnp.concatenate(grad_list, 0),
        totals[0],
        totals[1],
        totals[2],
        totals[3],
    )


def solution(mesh):
    return jax.shard_map(
        shards,
        mesh=mesh,
        in_specs=(
            P(("stream", "batch"), None, None, None),
            P("stream", None),
            P("stream"),
            P("stream", None),
            P("stream"),
            P(("stream", "batch"), None, None, None),
        ),
        out_specs=(
            P(("stream", "batch"), None, None, None),
            P(("stream", "batch"), None, None, None),
            P("stream", None),
            P("stream"),
            P("stream", None),
            P("stream"),
        ),
        check_vma=False,
    )
```

profile of v0, /device:TPU:0, one launch (start us, length us, event | category | flops | bytes accessed | tf_op | source)
XLA Modules:
  0.0 1994.7 jit_solution(5963125260289943411)
XLA Ops:
  55.5 21.2 %copy.318 = bf16[127,8,9,512]{3,1,2,0:T(8,128)(2,1)} copy(bf16[127,8,9,512]{3,2,1,0:T(8,128)(2,1)S(1)} %bitcast.365) | data formatting | bytes 18726912
  99.6 21.0 %copy.322 = bf16[127,8,9,512]{3,1,2,0:T(8,128)(2,1)} copy(bf16[127,8,9,512]{3,2,1,0:T(8,128)(2,1)S(1)} %bitcast.366) | data formatting | bytes 18726912
  132.4 20.8 %copy.320 = bf16[127,8,9,512]{3,1,2,0:T(8,128)(2,1)} copy(bf16[127,8,9,512]{3,2,1,0:T(8,128)(2,1)S(1)} %bitcast.367) | data formatting | bytes 18726912
  154.9 34.9 %all-reduce.25 = (bf16[1024]{0:T(1024)(128)(2,1)S(1)}, bf16[1024]{0:T(1024)(128)(2,1)S(1)}) all-reduce(bf16[1024]{0:T(1024)(128)(2,1)S(1)} %dynamic-update-slice.162, bf16[1024]{0:T(1024)(128)(2,1)S(1)} %dynamic-update-slice.163), channel_id=1, replica_groups=mesh['stream'=16,'batch'=2] {'stream'}, use_global_device_ids=true, to_apply=%add.20 | all-reduce | flops 2048 | bytes 8192
  251.6 20.8 %copy.321 = bf16[127,8,9,512]{3,1,2,0:T(8,128)(2,1)} copy(bf16[127,8,9,512]{3,2,1,0:T(8,128)(2,1)S(1)} %bitcast.368) | data formatting | bytes 18726912
  292.2 21.1 %copy.323 = bf16[127,8,9,512]{3,1,2,0:T(8,128)(2,1)} copy(bf16[127,8,9,512]{3,2,1,0:T(8,128)(2,1)S(1)} %bitcast.369) | data formatting | bytes 18726912
  333.1 21.1 %copy.319 = bf16[127,8,9,512]{3,1,2,0:T(8,128)(2,1)} copy(bf16[127,8,9,512]{3,2,1,0:T(8,128)(2,1)S(1)} %bitcast.364) | data formatting | bytes 18726912
  374.1 15.4 convert_reduce_fusion.2
  406.7 16.3 add_add_fusion
  430.0 15.3 fusion.48
  445.3 24.5 %reshape.2235 = f32[6,13,13,9,512]{4,3,2,1,0:T(8,128)} reshape(f32[1014,4608]{1,0:T(8,128)} %fusion.48) | data formatting | bytes 37380096 | tf_op jit(solution)/shard_map/reshape | solution.py:23
  469.8 54.8 %fusion.95 = (f32[6,13,13,1,512]{4,3,2,1,0:T(1,128)}, f32[6,13,13,1,512]{4,3,2,1,0:T(1,128)}, f32[6,13,13,1,512]{4,3,2,1,0:T(1,128)}, f32[6,13,13,1,512]{4,3,2,1...) fusion(f32[6,13,13,9,512]{4,3,2,1,0:T(8,128)} %reshape.2235), kind=kLoop, calls=%fused_computation.284 | loop fusion | bytes 37380096 | tf_op jit(solution)/shard_map/slice | solution.py:29
  529.9 15.5 scatter-add.241
  551.0 15.5 scatter-add.244
  570.2 14.2 scatter-add.245
  588.1 14.1 scatter-add.246
  606.0 14.1 scatter-add.249
  623.8 14.2 scatter-add.250
  689.7 23.7 %reshape.2189 = f32[6,13,13,9,512]{4,3,2,1,0:T(8,128)} reshape(f32[1014,4608]{1,0:T(8,128)} %fusion.52) | data formatting | bytes 37380096 | tf_op jit(solution)/shard_map/reshape | solution.py:23
  713.3 53.2 %fusion.91 = (f32[6,13,13,1,512]{4,3,2,1,0:T(1,128)}, f32[6,13,13,1,512]{4,3,2,1,0:T(1,128)}, f32[6,13,13,1,512]{4,3,2,1,0:T(1,128)}, f32[6,13,13,1,512]{4,3,2,1...) fusion(f32[6,13,13,9,512]{4,3,2,1,0:T(8,128)} %reshape.2189), kind=kLoop, calls=%fused_computation.280 | loop fusion | bytes 37380096 | tf_op jit(solution)/shard_map/slice | solution.py:29
  772.0 15.5 scatter-add.181
  793.0 15.4 scatter-add.184
  812.1 14.5 scatter-add.185
  830.4 14.1 scatter-add.186
  848.2 14.1 scatter-add.189
  931.6 23.7 %reshape.2214 = f32[6,13,13,9,512]{4,3,2,1,0:T(8,128)} reshape(f32[1014,4608]{1,0:T(8,128)} %fusion.50) | data formatting | bytes 37380096 | tf_op jit(solution)/shard_map/reshape | solution.py:23
  955.3 53.4 %fusion.93 = (f32[6,13,13,1,512]{4,3,2,1,0:T(1,128)}, f32[6,13,13,1,512]{4,3,2,1,0:T(1,128)}, f32[6,13,13,1,512]{4,3,2,1,0:T(1,128)}, f32[6,13,13,1,512]{4,3,2,1...) fusion(f32[6,13,13,9,512]{4,3,2,1,0:T(8,128)} %reshape.2214), kind=kLoop, calls=%fused_computation.282 | loop fusion | bytes 37380096 | tf_op jit(solution)/shard_map/slice | solution.py:29
  1014.1 15.5 scatter-add.211
  1035.1 15.4 scatter-add.214
  1189.5 16.3 add_add_fusion.1
  1218.8 30.0 %all-reduce.24 = (bf16[1024]{0:T(1024)(128)(2,1)S(1)}, bf16[1024]{0:T(1024)(128)(2,1)S(1)}) all-reduce(f32[1024]{0:T(1024)S(1)} %pad_select_fusion.3, f32[1024]{0:T(1024)S(1)} %pad_select_fusion.2), channel_id=3, replica_groups=mesh['stream'=16,'batch'=2] {'stream'}, use_global_device_ids=true, to_apply=%region_6.7.clone | all-reduce | flops 2048 | bytes 12288
  1266.8 23.9 %reshape.2245 = f32[6,13,13,9,512]{4,3,2,1,0:T(8,128)} reshape(f32[1014,4608]{1,0:T(8,128)} %fusion.60) | data formatting | bytes 37380096 | tf_op jit(solution)/shard_map/reshape | solution.py:23
  1290.7 55.0 %fusion.94 = (f32[6,13,13,1,512]{4,3,2,1,0:T(1,128)}, f32[6,13,13,1,512]{4,3,2,1,0:T(1,128)}, f32[6,13,13,1,512]{4,3,2,1,0:T(1,128)}, f32[6,13,13,1,512]{4,3,2,1...) fusion(f32[6,13,13,9,512]{4,3,2,1,0:T(8,128)} %reshape.2245), kind=kLoop, calls=%fused_computation.283 | loop fusion | bytes 37380096 | tf_op jit(solution)/shard_map/slice | solution.py:29
  1351.1 15.6 scatter-add.256
  1372.3 15.5 scatter-add.259
  1391.4 14.1 scatter-add.260
  1409.2 14.1 scatter-add.261
  1427.1 14.1 scatter-add.264
  1444.8 14.2 scatter-add.265
  1507.3 23.7 %reshape.2203 = f32[6,13,13,9,512]{4,3,2,1,0:T(8,128)} reshape(f32[1014,4608]{1,0:T(8,128)} %fusion.64) | data formatting | bytes 37380096 | tf_op jit(solution)/shard_map/reshape | solution.py:23
  1531.0 53.2 %fusion.90 = (f32[6,13,13,1,512]{4,3,2,1,0:T(1,128)}, f32[6,13,13,1,512]{4,3,2,1,0:T(1,128)}, f32[6,13,13,1,512]{4,3,2,1,0:T(1,128)}, f32[6,13,13,1,512]{4,3,2,1...) fusion(f32[6,13,13,9,512]{4,3,2,1,0:T(8,128)} %reshape.2203), kind=kLoop, calls=%fused_computation.279 | loop fusion | bytes 37380096 | tf_op jit(solution)/shard_map/slice | solution.py:29
  1589.6 15.5 scatter-add.196
  1610.6 15.4 scatter-add.199
  1629.7 14.3 scatter-add.200
  1745.7 23.7 %reshape.2224 = f32[6,13,13,9,512]{4,3,2,1,0:T(8,128)} reshape(f32[1014,4608]{1,0:T(8,128)} %fusion.62) | data formatting | bytes 37380096 | tf_op jit(solution)/shard_map/reshape | solution.py:23
  1769.3 53.5 %fusion.92 = (f32[6,13,13,1,512]{4,3,2,1,0:T(1,128)}, f32[6,13,13,1,512]{4,3,2,1,0:T(1,128)}, f32[6,13,13,1,512]{4,3,2,1,0:T(1,128)}, f32[6,13,13,1,512]{4,3,2,1...) fusion(f32[6,13,13,9,512]{4,3,2,1,0:T(8,128)} %reshape.2224), kind=kLoop, calls=%fused_computation.281 | loop fusion | bytes 37380096 | tf_op jit(solution)/shard_map/slice | solution.py:29
  1828.2 15.5 scatter-add.226
  1849.2 15.4 scatter-add.229
  (343 shorter events, 901.4 us)
Async XLA Ops:
  7.2 185.2 %all-gather.3.cloned.1.call-start = ((), (), s32[]{:S(2)}) async-start(), calls=%async_computation.2 | async-start | bytes 10027008 | tf_op jit(solution)/shard_map/all_gather | solution.py:64
  7.9 346.3 %all-gather.5.cloned.1.call-start = ((), (), s32[]{:S(2)}) async-start(), calls=%async_computation.3 | async-start | bytes 10027008 | tf_op jit(solution)/shard_map/all_gather | solution.py:70
  8.6 1927.1 %reduce-scatter.5.cloned.1.call-start = ((), (), s32[]{:S(2)}) async-start(), calls=%async_computation.5 | async-start | bytes 20054016 | tf_op jit(solution)/shard_map/reduce_scatter | solution.py:118
  29.7 3.1 copy-start.1
  34.4 4.3 copy-start.2
  132.3 20.8 %copy-start.30 = (u32[32]{0:T(128)S(1)}, u32[32]{0:T(128)}, u32[]{:S(2)}) copy-start(u32[32]{0:T(128)} %constant.1299) | copy-start | bytes 388
  132.3 22.1 %copy-start.37 = (bf16[64]{0:T(256)(128)(2,1)S(1)}, bf16[64]{0:T(256)(128)(2,1)}, u32[]{:S(2)}) copy-start(bf16[64]{0:T(256)(128)(2,1)} %param.116) | copy-start | bytes 388
  132.3 22.3 %copy-start.38 = (bf16[64]{0:T(256)(128)(2,1)S(1)}, bf16[64]{0:T(256)(128)(2,1)}, u32[]{:S(2)}) copy-start(bf16[64]{0:T(256)(128)(2,1)} %param.118) | copy-start | bytes 388
  132.4 59.3 %copy-start.35 = (s32[4]{0:T(128)S(1)}, s32[4]{0:T(128)}, u32[]{:S(2)}) copy-start(s32[4]{0:T(128)} %constant.1253.clone.1) | copy-start | bytes 52
  189.8 19.8 copy-start.28
  192.4 9.2 copy-start.3
  192.4 17.3 slice-start
  192.4 17.3 slice-start.1
  201.6 8.1 copy-start.18
  201.6 8.1 slice-start.2
  209.6 10.3 copy-start.19
  230.0 1.7 copy-start
  354.2 10.8 copy-start.36
  354.2 19.9 slice-start.9
  354.2 19.9 slice-start.10
  365.0 9.1 slice-start.11
  365.0 9.1 copy-start.20
  365.0 9.1 copy-start.21
  365.0 9.1 copy-start.31
  374.1 24.9 %slice-start.6 = ((s8[9363456]{0:T(1024)(128)(4,1)}), s8[974848]{0:T(1024)(128)(4,1)S(1)}, s32[]{:S(2)}) async-start(s8[9363456]{0:T(1024)(128)(4,1)} %bitcast.399), calls=%async_computation.13 | async-start | bytes 1949696
  374.1 24.9 %slice-start.7 = ((s8[9363456]{0:T(1024)(128)(4,1)}), s8[4194304]{0:T(1024)(128)(4,1)S(1)}, s32[]{:S(2)}) async-start(s8[9363456]{0:T(1024)(128)(4,1)} %bitcast.399), calls=%async_computation.14 | async-start | bytes 8388608
  389.6 9.4 slice-start.8
  389.6 9.4 copy-start.40
  399.0 7.6 copy-start.39
  429.9 1508.0 %reduce-scatter.3.cloned.1.call-start = ((), (), s32[]{:S(2)}) async-start(), calls=%async_computation.4 | async-start | bytes 20054016 | tf_op jit(solution)/shard_map/reduce_scatter | solution.py:116
  675.4 2.9 copy-start.42
  917.4 2.9 copy-start.41
  1159.1 3.0 copy-start.4
  1159.1 3.0 copy-start.29
  1162.0 19.8 slice-start.3
  1169.3 12.5 copy-start.24
  1169.3 12.4 copy-start.22
  1169.4 12.4 slice-start.4
  1169.4 12.4 slice-start.5
  1212.8 3.2 copy-start.27
  1212.8 4.6 copy-start.26
  1212.8 770.5 %all-reduce.30.cloned.1.call-start = ((), (), s32[]{:S(2)}) async-start(), calls=%async_computation.6 | async-start | bytes 2359296 | tf_op jit(solution)/shard_map/psum | solution.py:122
  1216.0 2.8 copy-start.32
  1216.0 2.8 copy-start.33
  1216.0 2.8 copy-start.34
  1975.8 1.7 copy-start.15
  1977.4 3.5 copy-start.16
  1977.4 3.5 copy-start.17
  (12 other events, 17.7 us)
Sparse Core Ops, SparseCore 0:
  10.3 84.1 all-gather.2
  96.7 79.7 all-gather.4
  430.0 192.0 reduce-scatter.4
  1212.9 192.2 reduce-scatter.2
  1940.3 40.3 all-reduce.29
where the time goes:
time: 2020 us; the launch traced here: 1990 us
  local copies, waits for them, and re-layouts  1470 us (73%)
  other arithmetic  231 us (11%)
  matrix products  205 us (10%)
  blocking collectives  69.8 us (3%)
    scatter-add x54, local copies, waits for them, and re-layouts, fold_rows(): padded.at[:, row_off:row_off + SIDE, col_off:col_off + SIDE, :]  695 us
    slice x6, local copies, waits for them, and re-layouts, fold_rows(): pieces[:, :, :, tap_index, :]  323 us
    unnamed x181, local copies, waits for them, and re-layouts  198 us
    add x42, other arithmetic, fold_rows(): padded.at[:, row_off:row_off + SIDE, col_off:col_off + SIDE, :]  154 us
    reshape x6, local copies, waits for them, and re-layouts, fold_rows(): pieces = grad_rows.reshape(image_count, SIDE, SIDE, 9, CH)  143 us
    another operation x14, local copies, waits for them, and re-layouts, patch_rows(): return jnp.stack(tap_list, 3).reshape(image_count * SIDE * SIDE, 9 * CH)  72.7 us
    dot_general x6, matrix products, back_rows(): lax.dot_general(grad_rows, weight, (((1,), (1,)), ((), ())), preferred_el...  72.5 us
    dot_general x6, matrix products, outer_sum(): lax.dot_general(left, right, (((0,), (0,)), ((), ())), preferred_element_...  69.6 us
  transfers between devices with their start and end apart: 5, of which 0 were waited for; matrix products, arithmetic and copies ran while one was open for 91% of the time, Pallas kernels for 0%

commit v1 on v0

v1 whole, which is shorter than its diff:
```python
import functools
import jax
import jax.numpy as jnp
import numpy as np
from jax import lax
from jax.experimental import pallas as pl
from jax.experimental.pallas import tpu as pltpu
from jax.sharding import PartitionSpec as P

CH = 512
SIDE = 13
ROOT = 0.7978845608
CUBE = 0.044715
f32 = jnp.float32
bf16 = jnp.bfloat16


def tanh_part(v, v2):
    return jnp.tanh(v * (ROOT + (ROOT * CUBE) * v2))


def gelu(v):
    half = 0.5 * v
    return half + half * tanh_part(v, v * v)


def gelu_both(v):
    v2 = v * v
    t = tanh_part(v, v2)
    half = 0.5 * v
    value = half + half * t
    slope = 0.5 + 0.5 * t + half * (1.0 - t * t) * (ROOT + (3 * ROOT * CUBE) * v2)
    return value, slope


def gelu_slope(v):
    return gelu_both(v)[1]


class Sizes:
    def __init__(self, clips):
        self.clips = clips
        self.used = clips * SIDE
        self.rows = -(-self.used // 16) * 16
        self.lanes = -(-self.rows // 256) * 256


def mask_rows(sz):
    row = np.arange(sz.rows)
    col = row % SIDE
    keep = row < sz.used
    table = np.stack([keep & (col != 0), keep, keep & (col != SIDE - 1)])
    return jnp.asarray(np.broadcast_to(table[:, :, None], (3, sz.rows, 128)), f32)


def spread(sz, dst, block, value, mask):
    rows = sz.rows
    where = pl.ds(pl.multiple_of(block * rows, 16), rows)
    for part in range(CH // 128):
        lane = part * 128
        x = value[:, lane : lane + 128]
        dst[where, lane : lane + 128] = (pltpu.roll(x, 1, 0) * mask[0]).astype(bf16)
        dst[where, CH + lane : CH + lane + 128] = (x * mask[1]).astype(bf16)
        dst[where, 2 * CH + lane : 2 * CH + lane + 128] = (
            pltpu.roll(x, rows - 1, 0) * mask[2]
        ).astype(bf16)


def turn(sz, dst, row, value, mask):
    kept = jnp.concatenate([value[:, k : k + 128] * mask[1] for k in range(0, CH, 128)], 1)
    full = jnp.concatenate([kept, jnp.zeros((sz.lanes - sz.rows, CH), f32)], 0).astype(bf16)
    dst[:, pl.ds(pl.multiple_of(row * sz.lanes, 128), sz.lanes)] = full.T


def flatten(sz, flat, stage):
    for n in range(sz.clips):
        flat[n * SIDE : (n + 1) * SIDE, :] = stage[n].astype(f32)


def unflatten(sz, stage, flat):
    for n in range(sz.clips):
        stage[n] = flat[n * SIDE : (n + 1) * SIDE, :].astype(bf16)


def fold8(value):
    return jnp.sum(value.reshape(value.shape[0] // 8, 8, CH), axis=0)


def rows13(product, finish, accs):
    accs[0][...] = product(0, skip=0)

    def pair(t, carry):
        i = 2 * t
        accs[1][...] = product(i + 1)
        finish(i, accs[0], 0)
        accs[0][...] = product(i + 2)
        finish(i + 1, accs[1], 1)
        return carry

    lax.fori_loop(0, 5, pair, 0)
    accs[1][...] = product(11)
    finish(10, accs[0], 0)
    accs[0][...] = product(12, skip=2)
    finish(11, accs[1], 1)
    finish(12, accs[0], 0)


def kernel(
    sz,
    images, cot, w4, w5, b4, b5, masks,
    out, igrad, dw4, dw5, db4, db5,
    pbuf, qbuf, xt, ht, pre4, acc0, acc1, flat_in, flat_out, stage_in, stage_out, in_sem, out_sem,
):
    rows, lanes = sz.rows, sz.lanes
    accs = (acc0, acc1)
    flats = (flat_in.at[0], flat_in.at[1])
    zero = jnp.zeros((rows, 3 * CH), bf16)
    for buf in (pbuf, qbuf):
        buf[0:rows, :] = zero
        buf[14 * rows : 15 * rows, :] = zero
        buf[15 * rows : 15 * rows + lanes - rows, :] = zero[: lanes - rows]
    flat_in[...] = jnp.zeros_like(flat_in)

    def fetch(src, i, slot):
        return pltpu.make_async_copy(src.at[:, i], stage_in.at[slot], in_sem.at[slot])

    def put(dst, i, slot):
        return pltpu.make_async_copy(stage_out.at[slot], dst.at[:, i], out_sem.at[slot])

    fetch(images, 0, 0).start()
    fetch(images, 1, 1).start()

    def prepare(i, slot):
        fetch(images, i, slot).wait()
        flatten(sz, flat_in.at[slot], stage_in.at[slot])
        fetch(images, jnp.minimum(i + 2, 12), slot).start()
        value = flat_in[slot]
        spread(sz, pbuf, i + 1, value, masks)
        turn(sz, xt, i, value, masks)

    def prepare_pair(t, carry):
        prepare(2 * t, 0)
        prepare(2 * t + 1, 1)
        return carry

    lax.fori_loop(0, 6, prepare_pair, 0)
    prepare(12, 0)
    fetch(images, 12, 1).wait()
    fetch(images, 12, 0).wait()

    fetch(cot, 0, 0).start()
    fetch(cot, 1, 1).start()

    def conv(src, w):
        def product(i, skip=None):
            total = None
            for a in range(3):
                if a == skip:
                    continue
                at = (i + a) * rows
                at = pl.multiple_of(at, 16)
                term = jnp.dot(
                    src[pl.ds(at, rows), :],
                    w[a * 3 * CH : (a + 1) * 3 * CH, :],
                    preferred_element_type=f32,
                )
                total = term if total is None else total + term
            return total

        return product

    def back(src, w):
        def product(i, skip=None):
            total = None
            for a in range(3):
                if skip is not None and a == 2 - skip:
                    continue
                at = pl.multiple_of((i + 2 - a) * rows, 16)
                for b in range(3):
                    tap = 3 * a + b
                    term = lax.dot_general(
                        src[pl.ds(at, rows), (2 - b) * CH : (3 - b) * CH],
                        w[tap * CH : (tap + 1) * CH, :],
                        (((1,), (1,)), ((), ())),
                        preferred_element_type=f32,
                    )
                    total = term if total is None else total + term
            return total

        return product

    def wgrad(left, src, dst):
        for a in range(3):

            def one(b, carry):
                total = None
                for q in range(13):
                    block = q + 2 - a
                    if block == 0 or block == 14:
                        continue
                    term = jnp.dot(
                        left[:, q * lanes : (q + 1) * lanes],
                        src[block * rows : block * rows + lanes,
                            pl.ds(pl.multiple_of((2 - b) * CH, CH), CH)],
                        preferred_element_type=f32,
                    )
                    total = term if total is None else total + term
                at = pl.multiple_of((3 * a + b) * CH, CH)
                dst[pl.ds(at, CH), :] = total.astype(dst.dtype)
                return carry

            lax.fori_loop(0, 3, one, 0)

    def finish4(i, acc, slot):
        v = acc[...] + b4[...]
        pre4[pl.ds(pl.multiple_of(i * rows, 16), rows), :] = v
        h = gelu(v)
        spread(sz, qbuf, i + 1, h, masks)
        turn(sz, ht, i, h, masks)

    rows13(conv(pbuf, w4), finish4, accs)

    put(out, 0, 0).start()
    put(out, 1, 1).start()
    db5[...] = jnp.zeros_like(db5)

    def finish5(i, acc, slot):
        put(out, i, slot).wait()
        fetch(cot, i, slot).wait()
        flatten(sz, flat_in.at[slot], stage_in.at[slot])
        fetch(cot, jnp.minimum(i + 2, 12), slot).start()
        value, slope = gelu_both(acc[...] + b5[...])
        flat_out[slot] = value
        unflatten(sz, stage_out.at[slot], flat_out.at[slot])
        put(out, i, slot).start()
        g = flat_in[slot] * slope
        g = g.astype(bf16).astype(f32)
        db5[...] += fold8(g)
        spread(sz, pbuf, i + 1, g, masks)

    rows13(conv(qbuf, w5), finish5, accs)
    fetch(cot, 12, 1).wait()
    fetch(cot, 12, 0).wait()

    wgrad(ht, pbuf, dw5)
    db4[...] = jnp.zeros_like(db4)

    def finish_back5(i, acc, slot):
        g = acc[...] * gelu_slope(pre4[pl.ds(pl.multiple_of(i * rows, 16), rows), :])
        g = jnp.concatenate([g[:, k : k + 128] * masks[1] for k in range(0, CH, 128)], 1)
        g = g.astype(bf16).astype(f32)
        db4[...] += fold8(g)
        spread(sz, qbuf, i + 1, g, masks)

    rows13(back(pbuf, w5), finish_back5, accs)
    wgrad(xt, qbuf, dw4)

    put(out, 12, 1).wait()
    put(out, 12, 0).wait()
    put(igrad, 0, 0).start()
    put(igrad, 1, 1).start()

    def finish_back4(i, acc, slot):
        put(igrad, i, slot).wait()
        flat_out[slot] = acc[...]
        unflatten(sz, stage_out.at[slot], flat_out.at[slot])
        put(igrad, i, slot).start()

    rows13(back(qbuf, w4), finish_back4, accs)
    put(igrad, 12, 1).wait()
    put(igrad, 12, 0).wait()


def block(images, cot, w4, w5, b4, b5):
    sz = Sizes(images.shape[0])
    rows, lanes = sz.rows, sz.lanes
    vm = pl.BlockSpec(memory_space=pltpu.VMEM)
    hb = pl.BlockSpec(memory_space=pl.ANY)
    return pl.pallas_call(
        functools.partial(kernel, sz),
        out_shape=(
            jax.ShapeDtypeStruct(images.shape, bf16),
            jax.ShapeDtypeStruct(images.shape, bf16),
            jax.ShapeDtypeStruct((9 * CH, CH), bf16),
            jax.ShapeDtypeStruct((9 * CH, CH), bf16),
            jax.ShapeDtypeStruct((8, CH), f32),
            jax.ShapeDtypeStruct((8, CH), f32),
        ),
        in_specs=[hb, hb, vm, vm, vm, vm, vm],
        out_specs=(hb, hb, vm, vm, vm, vm),
        scratch_shapes=[
            pltpu.VMEM((15 * rows + lanes - rows, 3 * CH), bf16),
            pltpu.VMEM((15 * rows + lanes - rows, 3 * CH), bf16),
            pltpu.VMEM((CH, SIDE * lanes), bf16),
            pltpu.VMEM((CH, SIDE * lanes), bf16),
            pltpu.VMEM((SIDE * rows, CH), f32),
            pltpu.VMEM((rows, CH), f32),
            pltpu.VMEM((rows, CH), f32),
            pltpu.VMEM((2, rows, CH), f32),
            pltpu.VMEM((2, rows, CH), f32),
            pltpu.VMEM((2, sz.clips, SIDE, CH), bf16),
            pltpu.VMEM((2, sz.clips, SIDE, CH), bf16),
            pltpu.SemaphoreType.DMA((2,)),
            pltpu.SemaphoreType.DMA((2,)),
        ],
        compiler_params=pltpu.CompilerParams(vmem_limit_bytes=63 << 20),
    )(images, cot, w4, w5, b4.reshape(1, CH).astype(f32), b5.reshape(1, CH).astype(f32), mask_rows(sz))


def shards(images, conv4_weight, conv4_bias, conv5_weight, conv5_bias, cotangent):
    half = lax.axis_size("stream") // 2
    group = lax.axis_index("stream") // half
    weights = lax.all_gather(
        jnp.concatenate([conv4_weight, conv5_weight], 1), "stream", axis=0, tiled=True
    )
    biases = lax.all_gather(jnp.stack([conv4_bias, conv5_bias], 1), "stream", axis=0, tiled=True)
    w4 = lax.dynamic_slice_in_dim(weights, group * CH, CH, 1)
    w5 = lax.dynamic_slice_in_dim(weights, (group + 2) * CH, CH, 1)
    own = lax.dynamic_slice_in_dim(biases, group * CH, CH, 0)
    out, igrad, dw4, dw5, db4, db5 = block(images, cotangent, w4, w5, own[:, 0], own[:, 1])

    def widen(value):
        value = value.astype(f32)
        blank = jnp.zeros_like(value)
        return jnp.where(
            group == 0,
            jnp.concatenate([value, blank], -1),
            jnp.concatenate([blank, value], -1),
        )

    def reduce(value):
        value = lax.psum_scatter(widen(value), "stream", scatter_dimension=0, tiled=True)
        return lax.psum(value.astype(bf16), "batch").astype(f32)

    dw4, dw5 = reduce(dw4), reduce(dw5)
    db = lax.psum(jnp.stack([widen(db4.sum(0)), widen(db5.sum(0))]), ("stream", "batch"))
    size = conv4_bias.shape[0]
    db = lax.dynamic_slice_in_dim(db, lax.axis_index("stream") * size, size, 1)
    return out, igrad, dw4, db[0], dw5, db[1]


def solution(mesh):
    clip = P(("stream", "batch"), None, None, None)
    weight = P("stream", None)
    bias = P("stream")
    return jax.shard_map(
        shards,
        mesh=mesh,
        in_specs=(clip, weight, bias, weight, bias, clip),
        out_specs=(clip, clip, weight, bias, weight, bias),
        check_vma=False,
    )
```

time: 2020 us -> 714 us (0.35); the launches traced: 1990 us -> 714 us
  local copies, waits for them, and re-layouts: 1470 us -> 8.65 us
  waiting for transfers between devices: 1.45 us -> 458 us
  matrix products: 205 us -> 0 us
  other arithmetic: 231 us -> 36.9 us
  Pallas kernels: 0 us -> 133 us
    scatter-add x54 -> x0, local copies, waits for them, and re-layouts: 695 us -> none  [fold_rows(): padded.at[:, row_off:row_off + SIDE, col_off:col_off + SIDE, :]]
    reduce_scatter x2, waiting for transfers between devices: 0.02 us -> 377 us  [reduce(): lax.psum_scatter(widen(value), 'stream', scatter_dimension=0, tiled=True)]
    slice x13 -> x0, local copies, waits for them, and re-layouts: 335 us -> none  [the longest x6 323 us: fold_rows(): pieces[:, :, :, tap_index, :]]
    dot_general x18 -> x0, matrix products: 205 us -> none  [the longest x6 72.5 us: back_rows(): lax.dot_general(grad_rows, weight, (((1,), (1,)), ((), ())), preferred_el...]
    unnamed x181 -> x5, local copies, waits for them, and re-layouts: 198 us -> 0.1 us
    reshape x18 -> x0, local copies, waits for them, and re-layouts: 168 us -> none  [the longest x6 143 us: fold_rows(): pieces = grad_rows.reshape(image_count, SIDE, SIDE, 9, CH)]
    add x44 -> x0, other arithmetic: 154 us -> none  [the longest x42 154 us: fold_rows(): padded.at[:, row_off:row_off + SIDE, col_off:col_off + SIDE, :]]
    pallas_call x0 -> x1, Pallas kernels: none -> 133 us  [block(): pl.pallas_call(functools.partial(kernel, sz), out_shape=(jax.ShapeDtypeSt...]
  transfers between devices with their start and end apart: 5 -> 4, of which waited for: 0 -> 4; matrix products, arithmetic and copies ran while one was open for 91% -> 3% of each run, Pallas kernels for 0% -> 0%
where the time goes in v1:
time: 714 us
  waiting for transfers between devices  458 us (64%)
  Pallas kernels  133 us (19%)
  blocking collectives  62.9 us (9%)
  other arithmetic  36.9 us (5%)
  between operations  13.9 us (2%)
  local copies, waits for them, and re-layouts  8.65 us (1%)
    reduce_scatter x2, waiting for transfers between devices, reduce(): lax.psum_scatter(widen(value), 'stream', scatter_dimension=0, tiled=True)  377 us
    pallas_call x1, Pallas kernels, block(): pl.pallas_call(functools.partial(kernel, sz), out_shape=(jax.ShapeDtypeSt...  133 us
    all_gather x1, waiting for transfers between devices, shards(): lax.all_gather(jnp.concatenate([conv4_weight, conv5_weight], 1), 'stream'...  77.7 us
    psum x1, blocking collectives, shards(): lax.psum(jnp.stack([widen(db4.sum(0)), widen(db5.sum(0))]), ('stream', 'b...  39.9 us
    all_gather x1, blocking collectives, shards(): lax.all_gather(jnp.stack([conv4_bias, conv5_bias], 1), 'stream', axis=0,...  23 us
    select_n x3, other arithmetic, widen(): jnp.where(group == 0, jnp.concatenate([value, blank], -1), jnp.concatenat...  17 us
  transfers between devices with their start and end apart: 4, of which 4 were waited for; matrix products, arithmetic and copies ran while one was open for 3% of the time, Pallas kernels for 0%

profile of v1, /device:TPU:0, one launch (start us, length us, event | category | flops | bytes accessed | tf_op | source)
XLA Modules:
  0.0 713.7 jit_solution(5994678150727776044)
XLA Ops:
  7.2 0.0 all-gather.3.cloned.1.call-start
  7.2 2.4 pad_maximum_fusion
  9.6 0.0 all-gather.3.cloned.1.call-update
  9.6 0.0 reduce-scatter.3.cloned.1.call-start
  9.7 0.7 maximum_bitcast_fusion
  10.4 23.0 %all-gather = bf16[16,64,2]{1,2,0:T(2,128)(2,1)S(1)} all-gather(bf16[1,64,2]{1,2,0:T(2,128)(2,1)S(1)} %maximum_bitcast_fusion), channel_id=1, replica_groups=mesh['stream'=16,'batch'=2] {'stream'}, dimensions={0}, use_global_device_ids=true | all-gather | bytes 4352 | tf_op jit(solution)/shard_map/all_gather | solution.py:316
  33.4 0.1 reshape.43
  33.5 0.7 fusion
  34.1 77.7 %all-gather.3.cloned.1.call-done = bf16[4608,2048]{1,0:T(8,128)(2,1)} async-done(((bf16[288,2048]{1,0:T(8,128)(2,1)}), bf16[4608,2048]{1,0:T(8,128)(2,1)}) %all-gather.3.cloned.1.call-update) | async-done | bytes 18874384 | tf_op jit(solution)/shard_map/all_gather | solution.py:313
  111.9 8.0 %constant_dynamic-slice_fusion.1 = (bf16[4608,512]{1,0:T(8,128)(2,1)}, bf16[4608,512]{1,0:T(8,128)(2,1)}) fusion(bf16[4608,2048]{1,0:T(8,128)(2,1)} %all-gather.3.cloned.1.call-done, s32[]{:T(128)S(6)} %select_n.43, s32[]{:T(128)S(6)} %select_n.42), kind=kLoop, calls=%fused_computation.11 | loop fusion | bytes 18874376 | tf_op jit(solution)/shard_map/dynamic_slice | solution.py:318
  119.8 133.1 %shard_map.118 = (bf16[18,13,13,512]{3,2,1,0:T(8,128)(2,1)}, bf16[18,13,13,512]{3,2,1,0:T(8,128)(2,1)}, bf16[4608,512]{1,0:T(8,128)(2,1)}, bf16[4608,512]{1,0:T(...) custom-call(bf16[18,13,13,512]{3,2,1,0:T(8,128)(2,1)} %images.1, bf16[18,13,13,512]{3,2,1,0:T(8,128)(2,1)} %cot.1, ...), custom_call_target="tpu_custom_call" | custom-call | tf_op jit(solution)/shard_map/pallas_call | solution.py:279
  252.9 3.7 convert_element_type.32
  256.6 7.0 pad_select_fusion.1
  263.6 0.0 reduce-scatter.3.cloned.1.call-update
  263.6 0.0 reduce-scatter.5.cloned.1.call-start
  263.7 3.7 convert_element_type.35
  267.3 10.1 %pad_select_fusion = f32[4608,1024]{1,0:T(8,128)} fusion(f32[4608,512]{1,0:T(8,128)S(1)} %convert_element_type.35, pred[]{:T(512)S(6)} %eq.2), kind=kLoop, calls=%fused_computation | loop fusion | flops 4718592 | bytes 28311552 | tf_op jit(solution)/shard_map/jit(_where)/select_n | solution.py:325
  277.4 0.0 reduce-scatter.5.cloned.1.call-update
  277.4 0.0 copy-start.1
  277.5 0.0 copy-start
  277.5 0.0 all-reduce.11.cloned.1.call-start
  277.5 181.2 %reduce-scatter.3.cloned.1.call-done = f32[288,1024]{1,0:T(8,128)} async-done(((f32[4608,1024]{1,0:T(8,128)}), f32[288,1024]{1,0:T(8,128)}) %reduce-scatter.3.cloned.1.call-update) | async-done | bytes 1179664 | tf_op jit(solution)/shard_map/reduce_scatter | solution.py:332
  458.7 2.2 convert_element_type.33
  460.9 195.9 %reduce-scatter.5.cloned.1.call-done = f32[288,1024]{1,0:T(8,128)} async-done(((f32[4608,1024]{1,0:T(8,128)}), f32[288,1024]{1,0:T(8,128)}) %reduce-scatter.5.cloned.1.call-update) | async-done | bytes 1179664 | tf_op jit(solution)/shard_map/reduce_scatter | solution.py:332
  656.8 2.2 convert_element_type.36
  659.0 0.0 all-reduce.11.cloned.1.call-update
  659.0 0.0 copy-done.1
  659.0 0.0 copy-done
  659.1 39.9 %psum.22 = f32[2,1024]{1,0:T(2,128)S(1)} all-reduce(f32[2,1024]{1,0:T(2,128)S(1)} %pad_maximum_fusion.1), channel_id=1, replica_groups=mesh['stream'=16,'batch'=2] {'stream','batch'}, use_global_device_ids=true, to_apply=%region_4.5 | all-reduce | flops 2048 | bytes 16384 | tf_op jit(solution)/shard_map/psum | solution.py:336
  699.0 0.1 constant_dynamic-slice_fusion
  699.0 0.5 slice_bitcast_fusion
  699.6 3.2 all-reduce.11.cloned.1.call-done
  702.8 2.2 convert_element_type.34
  705.0 2.2 convert_element_type.37
  (5 shorter events, 0.1 us)
Async XLA Ops:
  7.2 104.7 %all-gather.3.cloned.1.call-start = ((), (), s32[]{:S(2)}) async-start(), calls=%async_computation.2 | async-start | bytes 20054016 | tf_op jit(solution)/shard_map/all_gather | solution.py:313
  9.6 449.1 %reduce-scatter.3.cloned.1.call-start = ((), (), s32[]{:S(2)}) async-start(), calls=%async_computation.3 | async-start | bytes 20054016 | tf_op jit(solution)/shard_map/reduce_scatter | solution.py:332
  263.6 393.2 %reduce-scatter.5.cloned.1.call-start = ((), (), s32[]{:S(2)}) async-start(), calls=%async_computation.4 | async-start | bytes 20054016 | tf_op jit(solution)/shard_map/reduce_scatter | solution.py:332
  277.4 381.5 %copy-start.1 = (f32[8,512]{1,0:T(8,128)S(1)}, f32[8,512]{1,0:T(8,128)}, u32[]{:S(2)}) copy-start(f32[8,512]{1,0:T(8,128)} %get-tuple-element.15) | copy-start | bytes 49156
  277.5 381.6 %copy-start = (f32[8,512]{1,0:T(8,128)S(1)}, f32[8,512]{1,0:T(8,128)}, u32[]{:S(2)}) copy-start(f32[8,512]{1,0:T(8,128)} %get-tuple-element.16) | copy-start | bytes 49156
  277.5 425.3 %all-reduce.11.cloned.1.call-start = ((), (), s32[]{:S(2)}) async-start(), calls=%async_computation.5 | async-start | bytes 2359296 | tf_op jit(solution)/shard_map/psum | solution.py:333
Sparse Core Ops, SparseCore 0:
  10.2 101.6 all-gather.2
  263.7 194.9 reduce-scatter.2
  462.9 193.8 reduce-scatter.4
  659.6 43.1 all-reduce.10

commit v2 on v1

v2 whole, which is shorter than its diff:
```python
import functools
import jax
import jax.numpy as jnp
import numpy as np
from jax import lax
from jax.experimental import pallas as pl
from jax.experimental.pallas import tpu as pltpu
from jax.sharding import PartitionSpec as P

CH = 512
SIDE = 13
TAPS = 9
ROOT = 0.7978845608
CUBE = 0.044715
VMEM_LIMIT = 64 << 20
f32 = jnp.float32
bf16 = jnp.bfloat16
MESH = pl.DeviceIdType.MESH


def tanh_part(v, v2):
    return jnp.tanh(v * (ROOT + (ROOT * CUBE) * v2))


def gelu(v):
    half = 0.5 * v
    return half + half * tanh_part(v, v * v)


def gelu_both(v):
    v2 = v * v
    t = tanh_part(v, v2)
    half = 0.5 * v
    value = half + half * t
    slope = 0.5 + 0.5 * t + half * (1.0 - t * t) * (ROOT + (3 * ROOT * CUBE) * v2)
    return value, slope


class Sizes:
    def __init__(self, clips):
        self.clips = clips
        self.used = clips * SIDE
        self.rows = -(-self.used // 16) * 16
        self.lanes = -(-self.rows // 256) * 256
        self.tall = 15 * self.rows + self.lanes - self.rows


def mask_rows(sz):
    row = np.arange(sz.rows)
    col = row % SIDE
    keep = row < sz.used
    table = np.stack([keep & (col != 0), keep, keep & (col != SIDE - 1)])
    return jnp.asarray(np.broadcast_to(table[:, :, None], (3, sz.rows, 128)), f32)


def aligned(index, size):
    return pl.ds(pl.multiple_of(index * size, size), size)


def flatten(sz, flat, stage):
    for n in range(sz.clips):
        flat[n * SIDE : (n + 1) * SIDE, :] = stage[n].astype(f32)


def unflatten(sz, stage, flat):
    for n in range(sz.clips):
        stage[n] = flat[n * SIDE : (n + 1) * SIDE, :].astype(bf16)


def fold8(value):
    return jnp.sum(value.reshape(value.shape[0] // 8, 8, CH), axis=0)


def nothing(step):
    return None


class Work:
    def __init__(self, sz, images, cot, masks, out, igrad, bufs):
        self.sz = sz
        self.images, self.cot, self.out, self.igrad = images, cot, out, igrad
        self.masks = masks
        (self.pbuf, self.qbuf, self.xt, self.ht, self.pre4, acc0, acc1, self.flat_in,
         self.stage_in, self.stage_out, self.in_sem, self.out_sem) = bufs
        self.accs = (acc0, acc1)

    @staticmethod
    def buffers(sz):
        rows, lanes = sz.rows, sz.lanes
        return [
            pltpu.VMEM((sz.tall, 3 * CH), bf16),
            pltpu.VMEM((sz.tall, 3 * CH), bf16),
            pltpu.VMEM((CH, SIDE * lanes), bf16),
            pltpu.VMEM((CH, SIDE * lanes), bf16),
            pltpu.VMEM((SIDE * rows, CH), f32),
            pltpu.VMEM((rows, CH), f32),
            pltpu.VMEM((rows, CH), f32),
            pltpu.VMEM((2, rows, CH), f32),
            pltpu.VMEM((2, sz.clips, SIDE, CH), bf16),
            pltpu.VMEM((2, sz.clips, SIDE, CH), bf16),
            pltpu.SemaphoreType.DMA((2,)),
            pltpu.SemaphoreType.DMA((2,)),
        ]

    def clear(self):
        sz, rows = self.sz, self.sz.rows
        for buf in (self.pbuf, self.qbuf):
            buf[0:rows, :] = jnp.zeros((rows, 3 * CH), bf16)
            buf[14 * rows : sz.tall, :] = jnp.zeros((sz.tall - 14 * rows, 3 * CH), bf16)
        self.flat_in[...] = jnp.zeros_like(self.flat_in)

    def fetch(self, src, i, slot):
        return pltpu.make_async_copy(src.at[:, i], self.stage_in.at[slot], self.in_sem.at[slot])

    def put(self, dst, i, slot):
        return pltpu.make_async_copy(self.stage_out.at[slot], dst.at[:, i], self.out_sem.at[slot])

    def fetch_two(self, src):
        self.fetch(src, 0, 0).start()
        self.fetch(src, 1, 1).start()

    def fetch_end(self, src):
        self.fetch(src, 12, 1).wait()
        self.fetch(src, 12, 0).wait()

    def put_two(self, dst):
        self.put(dst, 0, 0).start()
        self.put(dst, 1, 1).start()

    def put_end(self, dst):
        self.put(dst, 12, 1).wait()
        self.put(dst, 12, 0).wait()

    def spread(self, dst, block, value):
        where = aligned(block, self.sz.rows)
        for lane in range(0, CH, 128):
            x = value[:, lane : lane + 128]
            left = pltpu.roll(x, 1, 0) * self.masks[0]
            right = pltpu.roll(x, self.sz.rows - 1, 0) * self.masks[2]
            dst[where, lane : lane + 128] = left.astype(bf16)
            dst[where, CH + lane : CH + lane + 128] = (x * self.masks[1]).astype(bf16)
            dst[where, 2 * CH + lane : 2 * CH + lane + 128] = right.astype(bf16)

    def kept(self, value):
        return jnp.concatenate([value[:, k : k + 128] * self.masks[1] for k in range(0, CH, 128)], 1)

    def turn(self, dst, i, value):
        sz = self.sz
        blank = jnp.zeros((sz.lanes - sz.rows, CH), f32)
        full = jnp.concatenate([self.kept(value), blank], 0).astype(bf16)
        dst[:, aligned(i, sz.lanes)] = full.T

    def prepare(self, i, slot):
        self.fetch(self.images, i, slot).wait()
        flatten(self.sz, self.flat_in.at[slot], self.stage_in.at[slot])
        self.fetch(self.images, jnp.minimum(i + 2, 12), slot).start()
        value = self.flat_in[slot]
        self.spread(self.pbuf, i + 1, value)
        self.turn(self.xt, i, value)

    def prepare_pairs(self, first, last):
        def pair(t, carry):
            self.prepare(2 * t, 0)
            self.prepare(2 * t + 1, 1)
            return carry

        lax.fori_loop(first, last, pair, 0)

    def rows13(self, product, finish, service=nothing):
        accs = self.accs
        accs[0][...] = product(0, 0)

        def pair(t, carry):
            i = 2 * t
            service(t)
            accs[1][...] = product(i + 1)
            finish(i, accs[0], 0)
            accs[0][...] = product(i + 2)
            finish(i + 1, accs[1], 1)
            return carry

        lax.fori_loop(0, 5, pair, 0)
        service(5)
        accs[1][...] = product(11)
        finish(10, accs[0], 0)
        service(6)
        accs[0][...] = product(12, 2)
        finish(11, accs[1], 1)
        finish(12, accs[0], 0)

    def partial_rows(self, product, store, service):
        def pair(t, carry):
            service(t)
            store(2 * t, product(2 * t))
            store(2 * t + 1, product(2 * t + 1))
            return carry

        lax.fori_loop(0, 6, pair, 0)
        store(12, product(12))

    def conv(self, src, w):
        rows = self.sz.rows

        def product(i, skip=None):
            total = None
            for a in range(3):
                if a == skip:
                    continue
                term = jnp.dot(
                    src[aligned(i + a, rows), :],
                    w[a * 3 * CH : (a + 1) * 3 * CH, :],
                    preferred_element_type=f32,
                )
                total = term if total is None else total + term
            return total

        return product

    def conv_taps(self, src, w, first, count):
        rows = self.sz.rows

        def product(i, skip=None):
            total = None
            for n in range(count):
                tap = first + n
                term = jnp.dot(
                    src[aligned(i + tap // 3, rows), aligned(tap % 3, CH)],
                    w[aligned(tap, CH), :],
                    preferred_element_type=f32,
                )
                total = term if total is None else total + term
            return total

        return product

    def back(self, src, w):
        rows = self.sz.rows

        def product(i, skip=None):
            total = None
            for a in range(3):
                if skip is not None and a == 2 - skip:
                    continue
                for b in range(3):
                    tap = 3 * a + b
                    term = lax.dot_general(
                        src[aligned(i + 2 - a, rows), (2 - b) * CH : (3 - b) * CH],
                        w[tap * CH : (tap + 1) * CH, :],
                        (((1,), (1,)), ((), ())),
                        preferred_element_type=f32,
                    )
                    total = term if total is None else total + term
            return total

        return product

    def wgrad(self, left, src, dst, service=nothing):
        rows, lanes = self.sz.rows, self.sz.lanes
        for a in range(3):

            def one(b, carry, a=a):
                total = None
                for q in range(13):
                    block = q + 2 - a
                    if block == 0 or block == 14:
                        continue
                    term = jnp.dot(
                        left[:, q * lanes : (q + 1) * lanes],
                        src[block * rows : block * rows + lanes, aligned(2 - b, CH)],
                        preferred_element_type=f32,
                    )
                    total = term if total is None else total + term
                dst[aligned(3 * a + b, CH), :] = total.astype(dst.dtype)
                service(3 * a + b)
                return carry

            lax.fori_loop(0, 3, one, 0)

    def finish4(self, b4):
        def finish(i, acc, slot):
            v = acc[...] + b4
            self.pre4[aligned(i, self.sz.rows), :] = v
            h = gelu(v)
            self.spread(self.qbuf, i + 1, h)
            self.turn(self.ht, i, h)

        return finish

    def finish5(self, b5, db5):
        def finish(i, acc, slot):
            self.put(self.out, i, slot).wait()
            self.fetch(self.cot, i, slot).wait()
            flatten(self.sz, self.flat_in.at[slot], self.stage_in.at[slot])
            self.fetch(self.cot, jnp.minimum(i + 2, 12), slot).start()
            value, slope = gelu_both(acc[...] + b5)
            acc[...] = value
            unflatten(self.sz, self.stage_out.at[slot], acc)
            self.put(self.out, i, slot).start()
            g = (self.flat_in[slot] * slope).astype(bf16).astype(f32)
            db5[...] += fold8(g)
            self.spread(self.pbuf, i + 1, g)

        return finish

    def finish_back5(self, db4):
        def finish(i, acc, slot):
            g = acc[...] * gelu_both(self.pre4[aligned(i, self.sz.rows), :])[1]
            g = self.kept(g).astype(bf16).astype(f32)
            db4[...] += fold8(g)
            self.spread(self.qbuf, i + 1, g)

        return finish

    def finish_back4(self, i, acc, slot):
        self.put(self.igrad, i, slot).wait()
        unflatten(self.sz, self.stage_out.at[slot], acc)
        self.put(self.igrad, i, slot).start()


def alone_kernel(sz, images, cot, w4, w5, b4, b5, masks, out, igrad, dw4, dw5, db4, db5, *bufs):
    work = Work(sz, images, cot, masks, out, igrad, bufs)
    work.clear()
    work.fetch_two(images)
    work.prepare_pairs(0, 6)
    work.prepare(12, 0)
    work.fetch_end(images)
    work.fetch_two(cot)
    work.rows13(work.conv(work.pbuf, w4), work.finish4(b4[...]))
    work.put_two(out)
    db5[...] = jnp.zeros_like(db5)
    work.rows13(work.conv(work.qbuf, w5), work.finish5(b5[...], db5))
    work.fetch_end(cot)
    work.wgrad(work.ht, work.pbuf, dw5)
    db4[...] = jnp.zeros_like(db4)
    work.rows13(work.back(work.pbuf, w5), work.finish_back5(db4))
    work.wgrad(work.xt, work.qbuf, dw4)
    work.put_end(out)
    work.put_two(igrad)
    work.rows13(work.back(work.qbuf, w4), work.finish_back4)
    work.put_end(igrad)


def block(images, cot, w4, w5, b4, b5):
    sz = Sizes(images.shape[0])
    vm = pl.BlockSpec(memory_space=pltpu.VMEM)
    hb = pl.BlockSpec(memory_space=pl.ANY)
    return pl.pallas_call(
        functools.partial(alone_kernel, sz),
        out_shape=(
            jax.ShapeDtypeStruct(images.shape, bf16),
            jax.ShapeDtypeStruct(images.shape, bf16),
            jax.ShapeDtypeStruct((TAPS * CH, CH), bf16),
            jax.ShapeDtypeStruct((TAPS * CH, CH), bf16),
            jax.ShapeDtypeStruct((8, CH), f32),
            jax.ShapeDtypeStruct((8, CH), f32),
        ),
        in_specs=[hb, hb, vm, vm, vm, vm, vm],
        out_specs=(hb, hb, vm, vm, vm, vm),
        scratch_shapes=Work.buffers(sz),
        compiler_params=pltpu.CompilerParams(vmem_limit_bytes=VMEM_LIMIT),
    )(images, cot, w4, w5, b4.reshape(1, CH).astype(f32), b5.reshape(1, CH).astype(f32), mask_rows(sz))


def plain_shards(images, conv4_weight, conv4_bias, conv5_weight, conv5_bias, cotangent):
    half = lax.axis_size("stream") // 2
    group = lax.axis_index("stream") // half
    weights = lax.all_gather(
        jnp.concatenate([conv4_weight, conv5_weight], 1), "stream", axis=0, tiled=True
    )
    biases = lax.all_gather(jnp.stack([conv4_bias, conv5_bias], 1), "stream", axis=0, tiled=True)
    w4 = lax.dynamic_slice_in_dim(weights, group * CH, CH, 1)
    w5 = lax.dynamic_slice_in_dim(weights, (group + 2) * CH, CH, 1)
    own = lax.dynamic_slice_in_dim(biases, group * CH, CH, 0)
    out, igrad, dw4, dw5, db4, db5 = block(images, cotangent, w4, w5, own[:, 0], own[:, 1])

    def widen(value):
        value = value.astype(f32)
        blank = jnp.zeros_like(value)
        return jnp.where(
            group == 0,
            jnp.concatenate([value, blank], -1),
            jnp.concatenate([blank, value], -1),
        )

    def reduce(value):
        value = lax.psum_scatter(widen(value), "stream", scatter_dimension=0, tiled=True)
        return lax.psum(value.astype(bf16), "batch").astype(f32)

    dw4, dw5 = reduce(dw4), reduce(dw5)
    db = lax.psum(jnp.stack([widen(db4.sum(0)), widen(db5.sum(0))]), ("stream", "batch"))
    size = conv4_bias.shape[0]
    db = lax.dynamic_slice_in_dim(db, lax.axis_index("stream") * size, size, 1)
    return out, igrad, dw4, db[0], dw5, db[1]


class Place:
    def __init__(self):
        s = lax.axis_index("stream")
        self.x = lax.axis_index("batch")
        self.c = s % 2
        self.y = (s // 2) % 2
        self.z = s // 4
        self.low = self.z % 2
        self.group = self.z // 2
        self.z1 = self.z + 1 - 2 * self.low
        self.z2 = (self.z + 2) % 4
        self.z12 = (self.z1 + 2) % 4
        self.number = self.x * 4 + self.y * 2 + self.low
        self.lead = self.c == self.x

    def device(self, x=None, y=None, z=None, c=None):
        x = self.x if x is None else x
        y = self.y if y is None else y
        z = self.z if z is None else z
        c = self.c if c is None else c
        return {"stream": (z * 2 + y) * 2 + c, "batch": x}

    def shard(self, k, c):
        z = (self.z, self.z1, self.z, self.z1, self.z2, self.z12, self.z2, self.z12)[k]
        y = self.y if k in (0, 1, 4, 5) else 1 - self.y
        return (z * 2 + y) * 2 + c

    def cube(self, m):
        return self.device(x=m // 4, y=(m // 2) % 2, z=self.group * 2 + m % 2)


def remote(src, dst, send, recv, device):
    return pltpu.make_async_remote_copy(
        src_ref=src, dst_ref=dst, send_sem=send, recv_sem=recv, device_id=device, device_id_type=MESH
    )


class Gather:
    SENDS = 29

    def __init__(self, at, given, full, sem_local, sends, recvs, cores):
        self.at, self.given, self.full = at, given, full
        self.sem_local, self.sends, self.recvs, self.cores = sem_local, sends, recvs, cores
        self.size = given.shape[0]
        self.cut = self.size // 3 // 16 * 16

    def rows(self, shard, part):
        start = (0, self.cut, 0)[part]
        size = (self.cut, self.size - self.cut, self.size)[part]
        return pl.ds(pl.multiple_of(shard * self.size + start, 16), size)

    def mine(self, part, group):
        start = (0, self.cut, 0)[part]
        size = (self.cut, self.size - self.cut, self.size)[part]
        return self.given.at[pl.ds(start, size), aligned(group, CH)]

    def ring(self, k):
        at = self.at
        zig, way = at.device(z=at.z1), at.device(y=1 - at.y)
        return {
            0: [(1, zig, 2), (2, way, 6)],
            1: [(3, way, 8)],
            4: [(5, zig, 4), (6, way, 10)],
            5: [(7, way, 12)],
        }.get(k, [])

    def copies(self, k, part):
        at = self.at
        spot = self.full.at[self.rows(at.shard(k, at.c), part), :]
        src = self.mine(part, at.group) if k == 0 else spot
        made = [
            remote(src, spot, self.sends.at[slot + part], self.recvs.at[there, part], device)
            for there, device, slot in self.ring(k)
        ]
        if k == 0:
            made.append(
                remote(
                    self.mine(part, 1 - at.group), spot,
                    self.sends.at[part], self.recvs.at[4, part], at.device(z=at.z2),
                )
            )
        if k > 0 and part == 1:
            made.append(
                remote(spot, spot, self.sends.at[13 + k], self.recvs.at[k, 1], at.device(x=1 - at.x))
            )
        return made

    def core(self, k):
        at = self.at
        spot = self.full.at[self.rows(at.shard(k, at.c), 2), :]
        src = self.mine(2, at.group) if k == 0 else spot
        return remote(src, spot, self.sends.at[21 + k], self.cores.at[k], at.device(c=1 - at.c))

    def local(self):
        at = self.at
        spot = self.full.at[self.rows(at.shard(0, at.c), 2), :]
        return pltpu.make_async_copy(self.mine(2, at.group), spot, self.sem_local)

    def begin(self):
        for copy in self.copies(0, 0):
            copy.start()

        @pl.when(self.at.lead)
        def _():
            for copy in self.copies(0, 1):
                copy.start()

        self.core(0).start()
        self.local().start()

    def arrived(self, k, part):
        at = self.at
        spot = self.full.at[self.rows(at.shard(k, at.c), part), :]
        return remote(spot, spot, self.sends.at[0], self.recvs.at[k, part], at.device(c=1 - at.c))

    def part_a(self, k):
        self.arrived(k, 0).wait_recv()
        for copy in self.copies(k, 0):
            copy.start()

    def part_b(self, k):
        self.arrived(k, 1).wait_recv()

        @pl.when(self.at.lead)
        def _():
            for copy in self.copies(k, 1):
                copy.start()

        self.core(k).start()

    def from_core(self, k):
        at = self.at
        spot = self.full.at[self.rows(at.shard(k, 1 - at.c), 2), :]
        remote(spot, spot, self.sends.at[0], self.cores.at[k], at.device(c=1 - at.c)).wait_recv()

    def near(self):
        self.local().wait()
        for k in range(4):
            self.from_core(k)

    def far(self):
        for k in range(4, 8):
            self.from_core(k)

    def sent(self):
        for k in range(8):
            for copy in self.copies(k, 0):
                copy.wait_send()
            self.core(k).wait_send()

        @pl.when(self.at.lead)
        def _():
            for k in range(8):
                for copy in self.copies(k, 1):
                    copy.wait_send()


class Scatter:
    def __init__(self, at, part, ebuf, fbuf, total, result, cross, sems):
        self.at, self.part, self.ebuf, self.fbuf, self.total, self.result = at, part, ebuf, fbuf, total, result
        self.cross = cross
        self.core_send, self.core_recv, self.far_send, self.far_recv, self.end_send, self.end_recv = sems
        self.size = ebuf.shape[1]
        self.half = self.size // 2

    def shard(self, j, c):
        return self.part.at[pl.ds(pl.multiple_of((2 * j + c) * self.size, 16), self.size), :]

    def core(self, j):
        at = self.at
        return remote(
            self.shard(j, 1 - at.c), self.ebuf.at[j], self.core_send.at[j], self.core_recv.at[j],
            at.device(c=1 - at.c),
        )

    def give(self, j):
        self.core(j).start()

    def out(self, j, h):
        at = self.at
        z, y = j // 2, j % 2
        to_z = at.group * 2 + z % 2
        kind = (z // 2 + at.group) % 2
        start = pl.multiple_of((2 * j + at.c) * self.size + h * self.half, 16)
        copy = remote(
            self.part.at[pl.ds(start, self.half), :], self.fbuf.at[kind, at.number],
            self.far_send.at[j, h], self.far_recv.at[kind, at.number],
            at.device(x=h, y=y, z=to_z),
        )
        away = (at.x + 2 * at.y + 4 * at.z) != (h + 2 * y + 4 * to_z)
        return copy, away

    def take(self, j):
        at = self.at
        self.core(j).wait_recv()
        start = pl.multiple_of((2 * j + at.c) * self.size, 16)
        where = pl.ds(start, self.size)
        self.part[where, :] = (self.part[where, :].astype(f32) + self.ebuf[j].astype(f32)).astype(bf16)
        for h in range(2):
            copy, away = self.out(j, h)
            pl.when(away)(copy.start)

    def tap(self, t):
        @pl.when(t >= 1)
        def _():
            self.give(t - 1)

        @pl.when(t >= 2)
        def _():
            self.take(t - 2)

    def sum_far(self):
        at = self.at
        for kind in range(2):
            z = at.z if kind == 0 else at.z2
            start = pl.multiple_of(((z * 2 + at.y) * 2 + at.c) * self.size + at.x * self.half, 16)
            self.total[kind] = self.part[pl.ds(start, self.half), :].astype(f32)

        def add(m, carry):
            @pl.when(m != at.number)
            def _():
                for kind in range(2):
                    spot = self.fbuf.at[kind, m]
                    remote(
                        spot, spot, self.far_send.at[0, 0], self.far_recv.at[kind, m], at.device(c=1 - at.c)
                    ).wait_recv()
                    self.total[kind] += spot[...].astype(f32)

            return carry

        lax.fori_loop(0, 8, add, 0)
        for kind in range(2):
            self.result[kind] = self.total[kind].astype(bf16)
        self.near_x().start()
        self.across().start()

    def near_x(self):
        at = self.at
        return remote(
            self.result.at[0], self.result.at[2], self.end_send.at[0], self.end_recv.at[0], at.device(x=1 - at.x)
        )

    def across(self):
        at = self.at
        return remote(
            self.result.at[1], self.cross, self.end_send.at[1], self.end_recv.at[1], at.device(z=at.z2)
        )

    def far_x(self):
        at = self.at
        return remote(
            self.cross, self.result.at[3], self.end_send.at[2], self.end_recv.at[2], at.device(x=1 - at.x)
        )

    def relay(self):
        self.across().wait_recv()
        self.far_x().start()

    def finish(self, dst):
        at = self.at
        self.near_x().wait_recv()
        self.far_x().wait_recv()
        for x, group, spot in (
            (at.x, at.group, self.result.at[0]),
            (1 - at.x, at.group, self.result.at[2]),
            (at.x, 1 - at.group, self.cross),
            (1 - at.x, 1 - at.group, self.result.at[3]),
        ):
            dst[aligned(x, self.half), aligned(group, CH)] = spot[...].astype(f32)
        self.near_x().wait_send()
        self.across().wait_send()
        self.far_x().wait_send()

    def sent(self):
        def one(j, carry):
            self.core(j).wait_send()
            for h in range(2):
                copy, away = self.out(j, h)
                pl.when(away)(copy.wait_send)
            return carry

        lax.fori_loop(0, 8, one, 0)


def cube_kernel(
    sz, images, cot, w4_in, w5_in, bias_in, masks, out, igrad, dw4, dw5, db, *scratch,
):
    bufs = scratch[:12]
    (w4, w5, part5, ebuf, fbuf, total, result, cross, bias, dbias, dsum,
     local_sem, gather_send, gather_recv, gather_core, core_send, core_recv, far_send, far_recv,
     end_send, end_recv, bias_send, bias_recv, db_send, db_recv, free_core, free_far) = scratch[12:]
    at = Place()
    work = Work(sz, images, cot, masks, out, igrad, bufs)
    gather = [
        Gather(at, given, full, local_sem.at[n], gather_send.at[n], gather_recv.at[n], gather_core.at[n])
        for n, (given, full) in enumerate(((w4_in, w4), (w5_in, w5)))
    ]
    sems = [
        (core_send.at[n], core_recv.at[n], far_send.at[n], far_recv.at[n], end_send.at[n], end_recv.at[n])
        for n in range(2)
    ]
    scatter5 = Scatter(at, part5, ebuf, fbuf, total, result, cross.at[0], sems[0])
    scatter4 = Scatter(at, w5, ebuf, fbuf, total, result, cross.at[1], sems[1])
    core = at.device(c=1 - at.c)

    barrier = pltpu.get_barrier_semaphore()

    def others(act):
        def one(m, carry):
            pl.when(m != at.number)(lambda: act(m))
            return carry

        lax.fori_loop(0, 8, one, 0)

    others(lambda m: pl.semaphore_signal(barrier, inc=1, device_id=at.cube(m), device_id_type=MESH))
    for device in (core, at.device(z=at.z2)):
        pl.semaphore_signal(barrier, inc=1, device_id=device, device_id_type=MESH)
    pl.semaphore_wait(barrier, 9)

    work.fetch_two(images)
    gather[0].begin()

    swap = remote(bias_in, bias.at[1], bias_send.at[0], bias_recv.at[0], core)
    swap.start()
    work.clear()
    work.prepare_pairs(0, 2)
    gather[0].part_a(1)
    gather[0].part_a(2)
    swap.wait_recv()
    slot = 2 + 2 * at.y + at.low
    bias[slot] = bias_in[...] + bias[1]

    def bias_way(n):
        y, z = ((1 - at.y, at.z), (at.y, at.z1), (1 - at.y, at.z1))[n]
        return remote(
            bias.at[slot], bias.at[slot], bias_send.at[1 + n], bias_recv.at[1 + n], at.device(y=y, z=z)
        )

    def bias_from(n):
        y, low = ((1 - at.y, at.low), (at.y, 1 - at.low), (1 - at.y, 1 - at.low))[n]
        spot = bias.at[2 + 2 * y + low]
        return remote(spot, spot, bias_send.at[1 + n], bias_recv.at[1 + n], core)

    for n in range(3):
        bias_way(n).start()
    gather[0].part_b(1)
    work.prepare_pairs(2, 4)
    gather[0].part_a(3)
    gather[0].part_b(2)
    work.prepare_pairs(4, 6)
    work.prepare(12, 0)
    work.fetch_end(images)
    work.fetch_two(cot)
    gather[0].part_b(3)
    for n in range(3):
        bias_from(n).wait_recv()
    gather[0].near()

    def far_steps(n, t):
        one = gather[n]

        def at_step(k, *acts):
            @pl.when(t == k)
            def _():
                for act, arg in acts:
                    act(arg)

        at_step(0, (one.part_a, 4), (one.part_b, 4))
        at_step(1, (one.part_a, 5))
        at_step(2, (one.part_b, 5))
        at_step(3, (one.part_a, 6))
        at_step(4, (one.part_b, 6), (one.part_a, 7))

    def near_steps(n, t):
        one = gather[n]

        def at_step(k, *acts):
            @pl.when(t == k)
            def _():
                for act, arg in acts:
                    act(arg)

        at_step(0, (one.part_a, 1), (one.part_a, 2))
        at_step(1, (one.part_b, 1))
        at_step(2, (one.part_a, 3))
        at_step(3, (one.part_b, 2))
        at_step(4, (one.part_b, 3))

    rows = sz.rows
    near_tap, far_tap = at.group * 5, (1 - at.group) * 4

    def store4(i, value):
        work.pre4[aligned(i, rows), :] = value

    work.partial_rows(work.conv_taps(work.pbuf, w4, near_tap, 4), store4, functools.partial(far_steps, 0))
    gather[0].part_b(7)
    gather[1].begin()
    gather[0].far()

    def rest4(i, skip=None):
        return work.conv_taps(work.pbuf, w4, far_tap, 5)(i) + work.pre4[aligned(i, rows), :]

    def bias_rows(n):
        return jnp.concatenate([bias[2 + m, n : n + 1, :] for m in (0, 2, 1, 3)], 1)

    work.rows13(rest4, work.finish4(bias_rows(0)), functools.partial(near_steps, 1))
    gather[1].near()

    def store5(i, value):
        high = value.astype(bf16)
        where = aligned(i + 1, rows)
        work.pbuf[where, 0:CH] = high
        work.pbuf[where, CH : 2 * CH] = (value - high.astype(f32)).astype(bf16)

    work.partial_rows(work.conv_taps(work.qbuf, w5, near_tap, 4), store5, functools.partial(far_steps, 1))
    gather[1].part_b(7)
    gather[1].far()

    def rest5(i, skip=None):
        where = aligned(i + 1, rows)
        kept = work.pbuf[where, 0:CH].astype(f32) + work.pbuf[where, CH : 2 * CH].astype(f32)
        return work.conv_taps(work.qbuf, w5, far_tap, 5)(i) + kept

    work.put_two(out)
    dbias[...] = jnp.zeros_like(dbias)
    db4, db5 = dbias.at[0, 0:8], dbias.at[0, 8:16]
    work.rows13(rest5, work.finish5(bias_rows(1), db5))
    work.fetch_end(cot)
    for one in gather:
        one.sent()
    swap.wait_send()
    for n in range(3):
        bias_way(n).wait_send()

    work.wgrad(work.ht, work.pbuf, part5, scatter5.tap)
    scatter5.take(7)
    pl.semaphore_signal(free_core, inc=1, device_id=core, device_id_type=MESH)

    def end_steps(one, t):
        @pl.when(t == 4)
        def _():
            one.sum_far()

        @pl.when(t == 6)
        def _():
            one.relay()

    work.rows13(work.back(work.pbuf, w5), work.finish_back5(db4), functools.partial(end_steps, scatter5))
    others(lambda m: pl.semaphore_signal(free_far, inc=1, device_id=at.cube(m), device_id_type=MESH))
    scatter5.finish(dw5)
    scatter5.sent()

    db_swap = remote(dbias.at[0], dbias.at[1], db_send.at[8], db_recv.at[8], core)
    db_swap.start()

    def db_way(m):
        return remote(dsum.at[at.number], dsum.at[at.number], db_send.at[m], db_recv.at[at.number], at.cube(m))

    def db_from(m):
        return remote(dsum.at[m], dsum.at[m], db_send.at[m], db_recv.at[m], at.cube(m))

    def tap4(t):
        @pl.when(t == 1)
        def _():
            pl.semaphore_wait(free_core, 1)

        @pl.when(t == 2)
        def _():
            pl.semaphore_wait(free_far, 7)

        @pl.when(t == 4)
        def _():
            db_swap.wait_recv()
            dsum[at.number] = dbias[0] + dbias[1]
            others(lambda m: db_way(m).start())

        scatter4.tap(t)

    work.wgrad(work.xt, work.qbuf, w5, tap4)
    scatter4.take(7)

    work.put_end(out)
    work.put_two(igrad)
    work.rows13(
        work.back(work.qbuf, w4), work.finish_back4, functools.partial(end_steps, scatter4)
    )
    others(lambda m: db_from(m).wait_recv())
    whole = dsum[0]
    for m in range(1, 8):
        whole = whole + dsum[m]
    db[0:1, :] = jnp.sum(whole[0:8], axis=0, keepdims=True)
    db[1:2, :] = jnp.sum(whole[8:16], axis=0, keepdims=True)
    db_swap.wait_send()
    others(lambda m: db_way(m).wait_send())
    work.put_end(igrad)
    scatter4.finish(dw4)
    scatter4.sent()


def cube_shards(images, conv4_weight, conv4_bias, conv5_weight, conv5_bias, cotangent):
    sz = Sizes(images.shape[0])
    size = conv4_weight.shape[0]
    stream = lax.axis_index("stream")
    pair = jnp.stack([conv4_bias, conv5_bias]).astype(f32)
    width = conv4_bias.shape[0]
    pair = jnp.pad(pair, ((0, 6), (0, 0)))
    blank = jnp.zeros_like(pair)
    pair = jnp.where(
        stream % 2 == 0, jnp.concatenate([pair, blank], 1), jnp.concatenate([blank, pair], 1)
    )
    vm = pl.BlockSpec(memory_space=pltpu.VMEM)
    hb = pl.BlockSpec(memory_space=pl.ANY)
    dma = pltpu.SemaphoreType.DMA
    out, igrad, dw4, dw5, db = pl.pallas_call(
        functools.partial(cube_kernel, sz),
        out_shape=(
            jax.ShapeDtypeStruct(images.shape, bf16),
            jax.ShapeDtypeStruct(images.shape, bf16),
            jax.ShapeDtypeStruct((size, 2 * CH), f32),
            jax.ShapeDtypeStruct((size, 2 * CH), f32),
            jax.ShapeDtypeStruct((2, CH), f32),
        ),
        in_specs=[hb, hb, hb, hb, vm, vm],
        out_specs=(hb, hb, vm, vm, vm),
        scratch_shapes=Work.buffers(sz)
        + [
            pltpu.VMEM((TAPS * CH, CH), bf16),
            pltpu.VMEM((TAPS * CH, CH), bf16),
            pltpu.VMEM((TAPS * CH, CH), bf16),
            pltpu.VMEM((8, size, CH), bf16),
            pltpu.VMEM((2, 8, size // 2, CH), bf16),
            pltpu.VMEM((2, size // 2, CH), f32),
            pltpu.VMEM((4, size // 2, CH), bf16),
            pltpu.VMEM((2, size // 2, CH), bf16),
            pltpu.VMEM((6, 8, 2 * width), f32),
            pltpu.VMEM((2, 16, CH), f32),
            pltpu.VMEM((8, 16, CH), f32),
            dma((2,)),
            dma((2, Gather.SENDS)),
            dma((2, 8, 2)),
            dma((2, 8)),
            dma((2, 8)),
            dma((2, 8)),
            dma((2, 8, 2)),
            dma((2, 2, 8)),
            dma((2, 3)),
            dma((2, 3)),
            dma((4,)),
            dma((4,)),
            dma((9,)),
            dma((9,)),
            pltpu.SemaphoreType.REGULAR,
            pltpu.SemaphoreType.REGULAR,
        ],
        compiler_params=pltpu.CompilerParams(
            vmem_limit_bytes=VMEM_LIMIT, collective_id=0, has_side_effects=True
        ),
    )(images, cotangent, conv4_weight, conv5_weight, pair, mask_rows(sz))
    own = lax.dynamic_slice_in_dim(db, stream * width % CH, width, 1)
    return out, igrad, dw4, own[0], dw5, own[1]


def solution(mesh):
    clip = P(("stream", "batch"), None, None, None)
    weight = P("stream", None)
    bias = P("stream")
    cube = dict(mesh.shape) == {"stream": 16, "batch": 2}
    return jax.shard_map(
        cube_shards if cube else plain_shards,
        mesh=mesh,
        in_specs=(clip, weight, bias, weight, bias, clip),
        out_specs=(clip, clip, weight, bias, weight, bias),
        check_vma=False,
    )
```

time: 714 us -> 222 us (0.31)
  the two profiles are of different devices: /device:TPU:0 before, /device:TPU:28 now
where the time goes in v2:
time: 222 us
  Pallas kernels  210 us (95%)
  local copies, waits for them, and re-layouts  9.97 us (4%)
    pallas_call x1, Pallas kernels, cube_shards(): pl.pallas_call(functools.partial(cube_kernel, sz), out_shape=(jax.ShapeDt...  210 us
    unnamed x10, local copies, waits for them, and re-layouts  8.71 us

profile of v2, /device:TPU:28, one launch (start us, length us, event | category | flops | bytes accessed | tf_op | source)
XLA Modules:
  0.0 221.6 jit_solution(6511494055215595006)
XLA Ops:
  0.7 0.7 fusion.3
  1.3 0.7 pad_select_fusion.bias_in
  2.0 209.6 %shard_map.118 = (bf16[18,13,13,512]{3,2,1,0:T(8,128)(2,1)}, bf16[18,13,13,512]{3,2,1,0:T(8,128)(2,1)}, f32[288,1024]{1,0:T(8,128)}, f32[288,1024]{1,0:T(8,128)}, f32[2,512]{1,0:T(2,128)}) custom-call(bf16[18,13,13,512]{3,2,1,0:T(8,128)(2,1)} %images.1, bf16[18,13,13,512]{3,2,1,0:T(8,128)(2,1)} %cot.1, bf16[288,1024]{1,0:T(8,128)(2,1)} %w4_in.1, ...), custom_call_target="tpu_custom_call" | custom-call | tf_op jit(solution)/shard_map/pallas_call | solution.py:909
  211.6 0.7 constant_dynamic-slice_fusion
  212.4 0.5 slice_bitcast_fusion
  212.9 0.0 copy-start
  212.9 4.6 %copy.17 = bf16[18,13,13,512]{3,2,1,0:T(8,128)(2,1)} copy(bf16[18,13,13,512]{3,2,1,0:T(8,128)(2,1)} %get-tuple-element.24) | data formatting | bytes 6230016
  217.5 0.0 copy-done
  217.5 0.0 copy-start.2
  217.5 0.0 copy-start.1
  217.5 2.0 copy.18
  219.4 0.1 copy-done.2
  219.6 1.0 copy.19
  220.6 0.0 copy-done.1
  220.6 1.0 copy.20
Async XLA Ops:
  212.9 4.6 %copy-start = (bf16[18,13,13,512]{3,2,1,0:T(8,128)(2,1)S(1)}, bf16[18,13,13,512]{3,2,1,0:T(8,128)(2,1)}, u32[]{:S(2)}) copy-start(bf16[18,13,13,512]{3,2,1,0:T(8,128)(2,1)} %get-tuple-element.25) | copy-start | bytes 9345028
  217.5 2.1 copy-start.2
  217.5 3.1 %copy-start.1 = (f32[288,1024]{1,0:T(8,128)S(1)}, f32[288,1024]{1,0:T(8,128)}, u32[]{:S(2)}) copy-start(f32[288,1024]{1,0:T(8,128)} %get-tuple-element.28) | copy-start | bytes 3538948

commit v3 on v2

--- a/solution.py
+++ b/solution.py
@@ -131,15 +131,16 @@
         self.put(dst, 12, 1).wait()
         self.put(dst, 12, 0).wait()
 
-    def spread(self, dst, block, value):
+    def spread(self, dst, block, value, flip=False):
+        low, high = (2 * CH, 0) if flip else (0, 2 * CH)
         where = aligned(block, self.sz.rows)
         for lane in range(0, CH, 128):
             x = value[:, lane : lane + 128]
             left = pltpu.roll(x, 1, 0) * self.masks[0]
             right = pltpu.roll(x, self.sz.rows - 1, 0) * self.masks[2]
-            dst[where, lane : lane + 128] = left.astype(bf16)
+            dst[where, low + lane : low + lane + 128] = left.astype(bf16)
             dst[where, CH + lane : CH + lane + 128] = (x * self.masks[1]).astype(bf16)
-            dst[where, 2 * CH + lane : 2 * CH + lane + 128] = right.astype(bf16)
+            dst[where, high + lane : high + lane + 128] = right.astype(bf16)
 
     def kept(self, value):
         return jnp.concatenate([value[:, k : k + 128] * self.masks[1] for k in range(0, CH, 128)], 1)
@@ -187,16 +188,6 @@
         accs[0][...] = product(12, 2)
         finish(11, accs[1], 1)
         finish(12, accs[0], 0)
-
-    def partial_rows(self, product, store, service):
-        def pair(t, carry):
-            service(t)
-            store(2 * t, product(2 * t))
-            store(2 * t + 1, product(2 * t + 1))
-            return carry
-
-        lax.fori_loop(0, 6, pair, 0)
-        store(12, product(12))
 
     def conv(self, src, w):
         rows = self.sz.rows
@@ -216,23 +207,6 @@
 
         return product
 
-    def conv_taps(self, src, w, first, count):
-        rows = self.sz.rows
-
-        def product(i, skip=None):
-            total = None
-            for n in range(count):
-                tap = first + n
-                term = jnp.dot(
-                    src[aligned(i + tap // 3, rows), aligned(tap % 3, CH)],
-                    w[aligned(tap, CH), :],
-                    preferred_element_type=f32,
-                )
-                total = term if total is None else total + term
-            return total
-
-        return product
-
     def back(self, src, w):
         rows = self.sz.rows
 
@@ -241,40 +215,37 @@
             for a in range(3):
                 if skip is not None and a == 2 - skip:
                     continue
-                for b in range(3):
-                    tap = 3 * a + b
-                    term = lax.dot_general(
-                        src[aligned(i + 2 - a, rows), (2 - b) * CH : (3 - b) * CH],
-                        w[tap * CH : (tap + 1) * CH, :],
-                        (((1,), (1,)), ((), ())),
-                        preferred_element_type=f32,
-                    )
-                    total = term if total is None else total + term
+                term = jnp.dot(
+                    src[aligned(i + 2 - a, rows), :],
+                    w[a * 3 * CH : (a + 1) * 3 * CH, :],
+                    preferred_element_type=f32,
+                )
+                total = term if total is None else total + term
             return total
 
         return product
 
-    def wgrad(self, left, src, dst, service=nothing):
+    def wgrad(self, left, src, w, dst, flip=None, service=nothing):
         rows, lanes = self.sz.rows, self.sz.lanes
-        for a in range(3):
-
-            def one(b, carry, a=a):
-                total = None
-                for q in range(13):
-                    block = q + 2 - a
-                    if block == 0 or block == 14:
-                        continue
-                    term = jnp.dot(
-                        left[:, q * lanes : (q + 1) * lanes],
-                        src[block * rows : block * rows + lanes, aligned(2 - b, CH)],
-                        preferred_element_type=f32,
-                    )
-                    total = term if total is None else total + term
-                dst[aligned(3 * a + b, CH), :] = total.astype(dst.dtype)
-                service(3 * a + b)
-                return carry
-
-            lax.fori_loop(0, 3, one, 0)
+
+        def one(t, carry):
+            tap = t if flip is None else t + flip * (TAPS - 1 - 2 * t)
+            a, b = tap // 3, tap % 3
+            total = None
+            for q in range(13):
+                start = pl.multiple_of((q + 2 - a) * rows, 16)
+                term = jnp.dot(
+                    left[:, q * lanes : (q + 1) * lanes],
+                    src[pl.ds(start, lanes), aligned(b, CH)],
+                    preferred_element_type=f32,
+                )
+                total = term if total is None else total + term
+            w[aligned(tap, CH), :] = w[aligned(tap, CH), :].T
+            dst[aligned(tap, CH), :] = total.astype(dst.dtype)
+            service(t)
+            return carry
+
+        lax.fori_loop(0, TAPS, one, 0)
 
     def finish4(self, b4):
         def finish(i, acc, slot):
@@ -298,7 +269,7 @@
             self.put(self.out, i, slot).start()
             g = (self.flat_in[slot] * slope).astype(bf16).astype(f32)
             db5[...] += fold8(g)
-            self.spread(self.pbuf, i + 1, g)
+            self.spread(self.pbuf, i + 1, g, True)
 
         return finish
 
@@ -307,7 +278,7 @@
             g = acc[...] * gelu_both(self.pre4[aligned(i, self.sz.rows), :])[1]
             g = self.kept(g).astype(bf16).astype(f32)
             db4[...] += fold8(g)
-            self.spread(self.qbuf, i + 1, g)
+            self.spread(self.qbuf, i + 1, g, True)
 
         return finish
 
@@ -317,7 +288,16 @@
         self.put(self.igrad, i, slot).start()
 
 
-def alone_kernel(sz, images, cot, w4, w5, b4, b5, masks, out, igrad, dw4, dw5, db4, db5, *bufs):
+def alone_kernel(
+    sz, images, cot, w4_in, w5_in, b4, b5, masks, out, igrad, dw4, dw5, db4, db5, *scratch,
+):
+    bufs, (w4, w5, sems) = scratch[:12], scratch[12:]
+    loads = [
+        pltpu.make_async_copy(src, dst, sems.at[n])
+        for n, (src, dst) in enumerate(((w4_in, w4), (w5_in, w5)))
+    ]
+    for load in loads:
+        load.start()
     work = Work(sz, images, cot, masks, out, igrad, bufs)
     work.clear()
     work.fetch_two(images)
@@ -325,15 +305,17 @@
     work.prepare(12, 0)
     work.fetch_end(images)
     work.fetch_two(cot)
+    for load in loads:
+        load.wait()
     work.rows13(work.conv(work.pbuf, w4), work.finish4(b4[...]))
     work.put_two(out)
     db5[...] = jnp.zeros_like(db5)
     work.rows13(work.conv(work.qbuf, w5), work.finish5(b5[...], db5))
     work.fetch_end(cot)
-    work.wgrad(work.ht, work.pbuf, dw5)
+    work.wgrad(work.ht, work.pbuf, w5, dw5)
     db4[...] = jnp.zeros_like(db4)
     work.rows13(work.back(work.pbuf, w5), work.finish_back5(db4))
-    work.wgrad(work.xt, work.qbuf, dw4)
+    work.wgrad(work.xt, work.qbuf, w4, dw4)
     work.put_end(out)
     work.put_two(igrad)
     work.rows13(work.back(work.qbuf, w4), work.finish_back4)
@@ -354,9 +336,14 @@
             jax.ShapeDtypeStruct((8, CH), f32),
             jax.ShapeDtypeStruct((8, CH), f32),
         ),
-        in_specs=[hb, hb, vm, vm, vm, vm, vm],
+        in_specs=[hb, hb, hb, hb, vm, vm, vm],
         out_specs=(hb, hb, vm, vm, vm, vm),
-        scratch_shapes=Work.buffers(sz),
+        scratch_shapes=Work.buffers(sz)
+        + [
+            pltpu.VMEM((TAPS * CH, CH), bf16),
+            pltpu.VMEM((TAPS * CH, CH), bf16),
+            pltpu.SemaphoreType.DMA((2,)),
+        ],
         compiler_params=pltpu.CompilerParams(vmem_limit_bytes=VMEM_LIMIT),
     )(images, cot, w4, w5, b4.reshape(1, CH).astype(f32), b5.reshape(1, CH).astype(f32), mask_rows(sz))
 
@@ -437,7 +424,7 @@
         self.at, self.given, self.full = at, given, full
         self.sem_local, self.sends, self.recvs, self.cores = sem_local, sends, recvs, cores
         self.size = given.shape[0]
-        self.cut = self.size // 3 // 16 * 16
+        self.cut = self.size * 2 // 7 // 16 * 16
 
     def rows(self, shard, part):
         start = (0, self.cut, 0)[part]
@@ -451,22 +438,17 @@
 
     def ring(self, k):
         at = self.at
-        zig, way = at.device(z=at.z1), at.device(y=1 - at.y)
-        return {
-            0: [(1, zig, 2), (2, way, 6)],
-            1: [(3, way, 8)],
-            4: [(5, zig, 4), (6, way, 10)],
-            5: [(7, way, 12)],
-        }.get(k, [])
+        ways = (at.device(y=1 - at.y, z=at.z1), at.device(z=at.z1), at.device(y=1 - at.y))
+        return [
+            (k + there, device, 2 + 2 * k // 4 * 3 + 2 * n)
+            for n, (there, device) in enumerate(zip((3, 1, 2), ways))
+        ]
 
     def copies(self, k, part):
         at = self.at
         spot = self.full.at[self.rows(at.shard(k, at.c), part), :]
         src = self.mine(part, at.group) if k == 0 else spot
-        made = [
-            remote(src, spot, self.sends.at[slot + part], self.recvs.at[there, part], device)
-            for there, device, slot in self.ring(k)
-        ]
+        made = []
         if k == 0:
             made.append(
                 remote(
@@ -474,6 +456,11 @@
                     self.sends.at[part], self.recvs.at[4, part], at.device(z=at.z2),
                 )
             )
+        if k in (0, 4):
+            made += [
+                remote(src, spot, self.sends.at[slot + part], self.recvs.at[there, part], device)
+                for there, device, slot in self.ring(k)
+            ]
         if k > 0 and part == 1:
             made.append(
                 remote(spot, spot, self.sends.at[13 + k], self.recvs.at[k, 1], at.device(x=1 - at.x))
@@ -508,33 +495,42 @@
         spot = self.full.at[self.rows(at.shard(k, at.c), part), :]
         return remote(spot, spot, self.sends.at[0], self.recvs.at[k, part], at.device(c=1 - at.c))
 
-    def part_a(self, k):
+    def first(self, k):
         self.arrived(k, 0).wait_recv()
         for copy in self.copies(k, 0):
             copy.start()
 
-    def part_b(self, k):
+    def rest(self, k):
+        self.lead(k)
+        self.follow(k)
+
+    def landed(self, k):
+        if k != 4:
+            self.arrived(k, 0).wait_recv()
         self.arrived(k, 1).wait_recv()
 
+    def lead(self, k):
         @pl.when(self.at.lead)
         def _():
+            self.landed(k)
             for copy in self.copies(k, 1):
                 copy.start()
-
-        self.core(k).start()
+            self.core(k).start()
+
+    def follow(self, k):
+        @pl.when(jnp.logical_not(self.at.lead))
+        def _():
+            self.landed(k)
+            self.core(k).start()
 
     def from_core(self, k):
         at = self.at
         spot = self.full.at[self.rows(at.shard(k, 1 - at.c), 2), :]
         remote(spot, spot, self.sends.at[0], self.cores.at[k], at.device(c=1 - at.c)).wait_recv()
 
-    def near(self):
+    def whole(self):
         self.local().wait()
-        for k in range(4):
-            self.from_core(k)
-
-    def far(self):
-        for k in range(4, 8):
+        for k in range(8):
             self.from_core(k)
 
     def sent(self):
@@ -556,7 +552,11 @@
         self.cross = cross
         self.core_send, self.core_recv, self.far_send, self.far_recv, self.end_send, self.end_recv = sems
         self.size = ebuf.shape[1]
+        self.flip = 1 - at.group
         self.half = self.size // 2
+
+    def pair(self, n):
+        return n + self.flip * (7 - 2 * n)
 
     def shard(self, j, c):
         return self.part.at[pl.ds(pl.multiple_of((2 * j + c) * self.size, 16), self.size), :]
@@ -568,8 +568,8 @@
             at.device(c=1 - at.c),
         )
 
-    def give(self, j):
-        self.core(j).start()
+    def give(self, n):
+        self.core(self.pair(n)).start()
 
     def out(self, j, h):
         at = self.at
@@ -585,8 +585,9 @@
         away = (at.x + 2 * at.y + 4 * at.z) != (h + 2 * y + 4 * to_z)
         return copy, away
 
-    def take(self, j):
-        at = self.at
+    def take(self, n):
+        at = self.at
+        j = self.pair(n)
         self.core(j).wait_recv()
         start = pl.multiple_of((2 * j + at.c) * self.size, 16)
         where = pl.ds(start, self.size)
@@ -604,30 +605,29 @@
         def _():
             self.take(t - 2)
 
-    def sum_far(self):
-        at = self.at
-        for kind in range(2):
-            z = at.z if kind == 0 else at.z2
-            start = pl.multiple_of(((z * 2 + at.y) * 2 + at.c) * self.size + at.x * self.half, 16)
-            self.total[kind] = self.part[pl.ds(start, self.half), :].astype(f32)
+    def sum_far(self, kind):
+        at = self.at
+        z = at.z if kind == 0 else at.z2
+        start = pl.multiple_of(((z * 2 + at.y) * 2 + at.c) * self.size + at.x * self.half, 16)
+        self.total[...] = self.part[pl.ds(start, self.half), :].astype(f32)
 
         def add(m, carry):
             @pl.when(m != at.number)
             def _():
-                for kind in range(2):
-                    spot = self.fbuf.at[kind, m]
-                    remote(
-                        spot, spot, self.far_send.at[0, 0], self.far_recv.at[kind, m], at.device(c=1 - at.c)
-                    ).wait_recv()
-                    self.total[kind] += spot[...].astype(f32)
+                spot = self.fbuf.at[kind, m]
+                remote(
+                    spot, spot, self.far_send.at[0, 0], self.far_recv.at[kind, m], at.device(c=1 - at.c)
+                ).wait_recv()
+                self.total[...] += spot[...].astype(f32)
 
             return carry
 
         lax.fori_loop(0, 8, add, 0)
-        for kind in range(2):
-            self.result[kind] = self.total[kind].astype(bf16)
-        self.near_x().start()
-        self.across().start()
+        self.result[kind] = self.total[...].astype(bf16)
+        if kind == 0:
+            self.near_x().start()
+        else:
+            self.across().start()
 
     def near_x(self):
         at = self.at
@@ -719,8 +719,7 @@
     swap.start()
     work.clear()
     work.prepare_pairs(0, 2)
-    gather[0].part_a(1)
-    gather[0].part_a(2)
+    gather[0].first(4)
     swap.wait_recv()
     slot = 2 + 2 * at.y + at.low
     bias[slot] = bias_in[...] + bias[1]
@@ -738,88 +737,52 @@
 
     for n in range(3):
         bias_way(n).start()
-    gather[0].part_b(1)
     work.prepare_pairs(2, 4)
-    gather[0].part_a(3)
-    gather[0].part_b(2)
+    gather[0].rest(1)
+    gather[0].rest(2)
+    gather[0].rest(3)
     work.prepare_pairs(4, 6)
     work.prepare(12, 0)
     work.fetch_end(images)
     work.fetch_two(cot)
-    gather[0].part_b(3)
+    gather[0].rest(4)
+    gather[1].begin()
     for n in range(3):
         bias_from(n).wait_recv()
-    gather[0].near()
-
-    def far_steps(n, t):
-        one = gather[n]
-
-        def at_step(k, *acts):
-            @pl.when(t == k)
-            def _():
-                for act, arg in acts:
-                    act(arg)
-
-        at_step(0, (one.part_a, 4), (one.part_b, 4))
-        at_step(1, (one.part_a, 5))
-        at_step(2, (one.part_b, 5))
-        at_step(3, (one.part_a, 6))
-        at_step(4, (one.part_b, 6), (one.part_a, 7))
-
-    def near_steps(n, t):
-        one = gather[n]
-
-        def at_step(k, *acts):
-            @pl.when(t == k)
-            def _():
-                for act, arg in acts:
-                    act(arg)
-
-        at_step(0, (one.part_a, 1), (one.part_a, 2))
-        at_step(1, (one.part_b, 1))
-        at_step(2, (one.part_a, 3))
-        at_step(3, (one.part_b, 2))
-        at_step(4, (one.part_b, 3))
-
-    rows = sz.rows
-    near_tap, far_tap = at.group * 5, (1 - at.group) * 4
-
-    def store4(i, value):
-        work.pre4[aligned(i, rows), :] = value
-
-    work.partial_rows(work.conv_taps(work.pbuf, w4, near_tap, 4), store4, functools.partial(far_steps, 0))
-    gather[0].part_b(7)
-    gather[1].begin()
-    gather[0].far()
-
-    def rest4(i, skip=None):
-        return work.conv_taps(work.pbuf, w4, far_tap, 5)(i) + work.pre4[aligned(i, rows), :]
+    for k in (5, 6, 7):
+        gather[0].rest(k)
+    gather[0].whole()
+
+    def steps(plan):
+        def service(t):
+            for k, acts in plan.items():
+                @pl.when(t == k)
+                def _(acts=acts):
+                    for act, *given in acts:
+                        act(*given)
+
+        return service
+
+    def gather_plan(one):
+        return steps({
+            0: [(one.first, 4), (one.lead, 1), (one.lead, 2)],
+            1: [(one.lead, 3), (one.follow, 1), (one.follow, 2)],
+            2: [(one.lead, 4), (one.follow, 3)],
+            3: [(one.lead, 5), (one.follow, 4)],
+            4: [(one.lead, 6), (one.lead, 7), (one.follow, 5)],
+            5: [(one.follow, 6), (one.follow, 7)],
+        })
 
     def bias_rows(n):
         return jnp.concatenate([bias[2 + m, n : n + 1, :] for m in (0, 2, 1, 3)], 1)
 
-    work.rows13(rest4, work.finish4(bias_rows(0)), functools.partial(near_steps, 1))
-    gather[1].near()
-
-    def store5(i, value):
-        high = value.astype(bf16)
-        where = aligned(i + 1, rows)
-        work.pbuf[where, 0:CH] = high
-        work.pbuf[where, CH : 2 * CH] = (value - high.astype(f32)).astype(bf16)
-
-    work.partial_rows(work.conv_taps(work.qbuf, w5, near_tap, 4), store5, functools.partial(far_steps, 1))
-    gather[1].part_b(7)
-    gather[1].far()
-
-    def rest5(i, skip=None):
-        where = aligned(i + 1, rows)
-        kept = work.pbuf[where, 0:CH].astype(f32) + work.pbuf[where, CH : 2 * CH].astype(f32)
-        return work.conv_taps(work.qbuf, w5, far_tap, 5)(i) + kept
+    work.rows13(work.conv(work.pbuf, w4), work.finish4(bias_rows(0)), gather_plan(gather[1]))
+    gather[1].whole()
 
     work.put_two(out)
     dbias[...] = jnp.zeros_like(dbias)
     db4, db5 = dbias.at[0, 0:8], dbias.at[0, 8:16]
-    work.rows13(rest5, work.finish5(bias_rows(1), db5))
+    work.rows13(work.conv(work.qbuf, w5), work.finish5(bias_rows(1), db5))
     work.fetch_end(cot)
     for one in gather:
         one.sent()
@@ -827,22 +790,16 @@
     for n in range(3):
         bias_way(n).wait_send()
 
-    work.wgrad(work.ht, work.pbuf, part5, scatter5.tap)
+    work.wgrad(work.ht, work.pbuf, w5, part5, scatter5.flip, scatter5.tap)
     scatter5.take(7)
     pl.semaphore_signal(free_core, inc=1, device_id=core, device_id_type=MESH)
 
-    def end_steps(one, t):
-        @pl.when(t == 4)
-        def _():
-            one.sum_far()
-
-        @pl.when(t == 6)
-        def _():
-            one.relay()
-
-    work.rows13(work.back(work.pbuf, w5), work.finish_back5(db4), functools.partial(end_steps, scatter5))
+    work.rows13(
+        work.back(work.pbuf, w5), work.finish_back5(db4),
+        steps({2: [(scatter5.sum_far, 1)], 6: [(scatter5.sum_far, 0)]}),
+    )
     others(lambda m: pl.semaphore_signal(free_far, inc=1, device_id=at.cube(m), device_id_type=MESH))
-    scatter5.finish(dw5)
+    scatter5.relay()
     scatter5.sent()
 
     db_swap = remote(dbias.at[0], dbias.at[1], db_send.at[8], db_recv.at[8], core)
@@ -861,6 +818,7 @@
 
         @pl.when(t == 2)
         def _():
+            scatter5.finish(dw5)
             pl.semaphore_wait(free_far, 7)
 
         @pl.when(t == 4)
@@ -871,13 +829,18 @@
 
         scatter4.tap(t)
 
-    work.wgrad(work.xt, work.qbuf, w5, tap4)
+    work.wgrad(work.xt, work.qbuf, w4, w5, scatter4.flip, tap4)
     scatter4.take(7)
 
     work.put_end(out)
     work.put_two(igrad)
     work.rows13(
-        work.back(work.qbuf, w4), work.finish_back4, functools.partial(end_steps, scatter4)
+        work.back(work.qbuf, w4), work.finish_back4,
+        steps({
+            2: [(scatter4.sum_far, 1)],
+            4: [(scatter4.relay,)],
+            5: [(scatter4.sum_far, 0)],
+        }),
     )
     others(lambda m: db_from(m).wait_recv())
     whole = dsum[0]
@@ -924,7 +887,7 @@
             pltpu.VMEM((TAPS * CH, CH), bf16),
             pltpu.VMEM((8, size, CH), bf16),
             pltpu.VMEM((2, 8, size // 2, CH), bf16),
-            pltpu.VMEM((2, size // 2, CH), f32),
+            pltpu.VMEM((size // 2, CH), f32),
             pltpu.VMEM((4, size // 2, CH), bf16),
             pltpu.VMEM((2, size // 2, CH), bf16),
             pltpu.VMEM((6, 8, 2 * width), f32),

time: 222 us -> 212 us (0.955)
  the two profiles are of different devices: /device:TPU:28 before, /device:TPU:0 now
where the time goes in v3:
time: 212 us
  Pallas kernels  200 us (94%)
  local copies, waits for them, and re-layouts  9.98 us (5%)
    pallas_call x1, Pallas kernels, cube_shards(): pl.pallas_call(functools.partial(cube_kernel, sz), out_shape=(jax.ShapeDt...  200 us
    unnamed x10, local copies, waits for them, and re-layouts  8.71 us

profile of v3, /device:TPU:0, one launch (start us, length us, event | category | flops | bytes accessed | tf_op | source)
XLA Modules:
  0.0 212.0 jit_solution(2387222169770951863)
XLA Ops:
  0.7 0.7 fusion.3
  1.3 0.7 pad_select_fusion.bias_in
  2.0 200.0 %shard_map.118 = (bf16[18,13,13,512]{3,2,1,0:T(8,128)(2,1)}, bf16[18,13,13,512]{3,2,1,0:T(8,128)(2,1)}, f32[288,1024]{1,0:T(8,128)}, f32[288,1024]{1,0:T(8,128)}, f32[2,512]{1,0:T(2,128)}) custom-call(bf16[18,13,13,512]{3,2,1,0:T(8,128)(2,1)} %images.1, bf16[18,13,13,512]{3,2,1,0:T(8,128)(2,1)} %cot.1, bf16[288,1024]{1,0:T(8,128)(2,1)} %w4_in.1, ...), custom_call_target="tpu_custom_call" | custom-call | tf_op jit(solution)/shard_map/pallas_call | solution.py:872
  202.0 0.8 constant_dynamic-slice_fusion
  202.7 0.5 slice_bitcast_fusion
  203.3 0.0 copy-start
  203.3 4.6 %copy.17 = bf16[18,13,13,512]{3,2,1,0:T(8,128)(2,1)} copy(bf16[18,13,13,512]{3,2,1,0:T(8,128)(2,1)} %get-tuple-element.24) | data formatting | bytes 6230016
  207.8 0.0 copy-done
  207.9 0.0 copy-start.2
  207.9 0.0 copy-start.1
  207.9 2.0 copy.18
  209.8 0.1 copy-done.2
  210.0 1.0 copy.19
  211.0 0.0 copy-done.1
  211.0 1.0 copy.20
Async XLA Ops:
  203.3 4.6 %copy-start = (bf16[18,13,13,512]{3,2,1,0:T(8,128)(2,1)S(1)}, bf16[18,13,13,512]{3,2,1,0:T(8,128)(2,1)}, u32[]{:S(2)}) copy-start(bf16[18,13,13,512]{3,2,1,0:T(8,128)(2,1)} %get-tuple-element.25) | copy-start | bytes 9345028
  207.9 2.1 copy-start.2
  207.9 3.1 %copy-start.1 = (f32[288,1024]{1,0:T(8,128)S(1)}, f32[288,1024]{1,0:T(8,128)}, u32[]{:S(2)}) copy-start(f32[288,1024]{1,0:T(8,128)} %get-tuple-element.28) | copy-start | bytes 3538948

commit v4 on v3

--- a/solution.py
+++ b/solution.py
@@ -43,6 +43,7 @@
         self.rows = -(-self.used // 16) * 16
         self.lanes = -(-self.rows // 256) * 256
         self.tall = 15 * self.rows + self.lanes - self.rows
+        self.step = 8 * max(n for n in range(1, 11) if self.rows // 8 % n == 0)
 
 
 def mask_rows(sz):
@@ -68,7 +69,11 @@
 
 
 def fold8(value):
-    return jnp.sum(value.reshape(value.shape[0] // 8, 8, CH), axis=0)
+    return jnp.sum(value.reshape(value.shape[0] // 8, 8, 128), axis=0)
+
+
+def columns():
+    return [slice(lane, lane + 128) for lane in range(0, CH, 128)]
 
 
 def nothing(step):
@@ -131,33 +136,35 @@
         self.put(dst, 12, 1).wait()
         self.put(dst, 12, 0).wait()
 
-    def spread(self, dst, block, value, flip=False):
+    def spread(self, dst, block, cols, x, flip=False):
         low, high = (2 * CH, 0) if flip else (0, 2 * CH)
-        where = aligned(block, self.sz.rows)
-        for lane in range(0, CH, 128):
-            x = value[:, lane : lane + 128]
-            left = pltpu.roll(x, 1, 0) * self.masks[0]
-            right = pltpu.roll(x, self.sz.rows - 1, 0) * self.masks[2]
-            dst[where, low + lane : low + lane + 128] = left.astype(bf16)
-            dst[where, CH + lane : CH + lane + 128] = (x * self.masks[1]).astype(bf16)
-            dst[where, high + lane : high + lane + 128] = right.astype(bf16)
-
-    def kept(self, value):
-        return jnp.concatenate([value[:, k : k + 128] * self.masks[1] for k in range(0, CH, 128)], 1)
-
-    def turn(self, dst, i, value):
+        where, lane = aligned(block, self.sz.rows), cols.start
+        left = pltpu.roll(x, 1, 0) * self.masks[0]
+        right = pltpu.roll(x, self.sz.rows - 1, 0) * self.masks[2]
+        dst[where, low + lane : low + lane + 128] = left.astype(bf16)
+        dst[where, CH + lane : CH + lane + 128] = (x * self.masks[1]).astype(bf16)
+        dst[where, high + lane : high + lane + 128] = right.astype(bf16)
+
+    def steps(self):
+        return [slice(r, r + self.sz.step) for r in range(0, self.sz.rows, self.sz.step)]
+
+    def within(self, i, some):
+        start = pl.multiple_of(i * self.sz.rows, 16) + some.start
+        return pl.ds(pl.multiple_of(start, 8), self.sz.step)
+
+    def turn(self, dst, src, i):
         sz = self.sz
-        blank = jnp.zeros((sz.lanes - sz.rows, CH), f32)
-        full = jnp.concatenate([self.kept(value), blank], 0).astype(bf16)
-        dst[:, aligned(i, sz.lanes)] = full.T
+        value = src[aligned(i + 1, sz.rows), CH : 2 * CH]
+        blank = jnp.zeros((sz.lanes - sz.rows, CH), bf16)
+        dst[:, aligned(i, sz.lanes)] = jnp.concatenate([value, blank], 0).T
 
     def prepare(self, i, slot):
         self.fetch(self.images, i, slot).wait()
         flatten(self.sz, self.flat_in.at[slot], self.stage_in.at[slot])
         self.fetch(self.images, jnp.minimum(i + 2, 12), slot).start()
-        value = self.flat_in[slot]
-        self.spread(self.pbuf, i + 1, value)
-        self.turn(self.xt, i, value)
+        for cols in columns():
+            self.spread(self.pbuf, i + 1, cols, self.flat_in[slot, :, cols])
+        self.turn(self.xt, self.pbuf, i)
 
     def prepare_pairs(self, first, last):
         def pair(t, carry):
@@ -206,6 +213,30 @@
             return total
 
         return product
+
+    def lot(self, src, w, taps):
+        rows = self.sz.rows
+
+        def product(i, skip=None):
+            total = None
+            for a in taps:
+                term = jnp.dot(
+                    src[aligned(i + a, rows), :], w[aligned(a, 3 * CH), :], preferred_element_type=f32
+                )
+                total = term if total is None else total + term
+            return total
+
+        return product
+
+    def each(self, product, store, service=nothing):
+        def pair(t, carry):
+            service(t)
+            store(2 * t, product(2 * t))
+            store(2 * t + 1, product(2 * t + 1))
+            return carry
+
+        lax.fori_loop(0, 6, pair, 0)
+        store(12, product(12))
 
     def back(self, src, w):
         rows = self.sz.rows
@@ -249,11 +280,14 @@
 
     def finish4(self, b4):
         def finish(i, acc, slot):
-            v = acc[...] + b4
-            self.pre4[aligned(i, self.sz.rows), :] = v
-            h = gelu(v)
-            self.spread(self.qbuf, i + 1, h)
-            self.turn(self.ht, i, h)
+            for cols in columns():
+                parts = []
+                for some in self.steps():
+                    v = acc[some, cols] + b4[:, cols]
+                    self.pre4[self.within(i, some), cols] = v
+                    parts.append(gelu(v))
+                self.spread(self.qbuf, i + 1, cols, jnp.concatenate(parts, 0))
+            self.turn(self.ht, self.qbuf, i)
 
         return finish
 
@@ -263,22 +297,33 @@
             self.fetch(self.cot, i, slot).wait()
             flatten(self.sz, self.flat_in.at[slot], self.stage_in.at[slot])
             self.fetch(self.cot, jnp.minimum(i + 2, 12), slot).start()
-            value, slope = gelu_both(acc[...] + b5)
-            acc[...] = value
+            for cols in columns():
+                parts, total = [], db5[:, cols]
+                for some in self.steps():
+                    value, slope = gelu_both(acc[some, cols] + b5[:, cols])
+                    acc[some, cols] = value
+                    g = (self.flat_in[slot, some, cols] * slope).astype(bf16).astype(f32)
+                    total = total + fold8(g)
+                    parts.append(g)
+                db5[:, cols] = total
+                self.spread(self.pbuf, i + 1, cols, jnp.concatenate(parts, 0), True)
             unflatten(self.sz, self.stage_out.at[slot], acc)
             self.put(self.out, i, slot).start()
-            g = (self.flat_in[slot] * slope).astype(bf16).astype(f32)
-            db5[...] += fold8(g)
-            self.spread(self.pbuf, i + 1, g, True)
 
         return finish
 
     def finish_back5(self, db4):
         def finish(i, acc, slot):
-            g = acc[...] * gelu_both(self.pre4[aligned(i, self.sz.rows), :])[1]
-            g = self.kept(g).astype(bf16).astype(f32)
-            db4[...] += fold8(g)
-            self.spread(self.qbuf, i + 1, g, True)
+            for cols in columns():
+                parts, total = [], db4[:, cols]
+                for some in self.steps():
+                    slope = gelu_both(self.pre4[self.within(i, some), cols])[1]
+                    g = acc[some, cols] * slope * self.masks[1, some, :]
+                    g = g.astype(bf16).astype(f32)
+                    total = total + fold8(g)
+                    parts.append(g)
+                db4[:, cols] = total
+                self.spread(self.qbuf, i + 1, cols, jnp.concatenate(parts, 0), True)
 
         return finish
 
@@ -528,9 +573,13 @@
         spot = self.full.at[self.rows(at.shard(k, 1 - at.c), 2), :]
         remote(spot, spot, self.sends.at[0], self.cores.at[k], at.device(c=1 - at.c)).wait_recv()
 
-    def whole(self):
+    def near(self):
         self.local().wait()
-        for k in range(8):
+        for k in range(4):
+            self.from_core(k)
+
+    def far(self):
+        for k in range(4, 8):
             self.from_core(k)
 
     def sent(self):
@@ -749,9 +798,7 @@
     gather[1].begin()
     for n in range(3):
         bias_from(n).wait_recv()
-    for k in (5, 6, 7):
-        gather[0].rest(k)
-    gather[0].whole()
+    gather[0].near()
 
     def steps(plan):
         def service(t):
@@ -763,26 +810,56 @@
 
         return service
 
-    def gather_plan(one):
-        return steps({
-            0: [(one.first, 4), (one.lead, 1), (one.lead, 2)],
-            1: [(one.lead, 3), (one.follow, 1), (one.follow, 2)],
-            2: [(one.lead, 4), (one.follow, 3)],
-            3: [(one.lead, 5), (one.follow, 4)],
-            4: [(one.lead, 6), (one.lead, 7), (one.follow, 5)],
-            5: [(one.follow, 6), (one.follow, 7)],
-        })
-
     def bias_rows(n):
         return jnp.concatenate([bias[2 + m, n : n + 1, :] for m in (0, 2, 1, 3)], 1)
 
-    work.rows13(work.conv(work.pbuf, w4), work.finish4(bias_rows(0)), gather_plan(gather[1]))
-    gather[1].whole()
+    rows = sz.rows
+    near_row, far_row = 2 * at.group, 2 - 2 * at.group
+
+    def keep4(i, value):
+        work.pre4[aligned(i, rows), :] = value
+
+    def rest4(i, skip=None):
+        kept = work.pre4[aligned(i, rows), :]
+        return kept + work.lot(work.pbuf, w4, (1, far_row))(i)
+
+    def keep5(i, value):
+        high = value.astype(bf16)
+        where = aligned(i + 1, rows)
+        work.pbuf[where, 0:CH] = high
+        work.pbuf[where, CH : 2 * CH] = (value - high.astype(f32)).astype(bf16)
+
+    def rest5(i, skip=None):
+        where = aligned(i + 1, rows)
+        kept = work.pbuf[where, 0:CH].astype(f32) + work.pbuf[where, CH : 2 * CH].astype(f32)
+        return kept + work.lot(work.qbuf, w5, (1, far_row))(i)
+
+    w4_way, w5_way = gather
+    work.each(work.lot(work.pbuf, w4, (near_row,)), keep4, steps({
+        1: [(w4_way.lead, 5)],
+        2: [(w4_way.lead, 6), (w4_way.follow, 5)],
+        3: [(w4_way.lead, 7), (w4_way.follow, 6)],
+        4: [(w4_way.follow, 7)],
+        5: [(w5_way.first, 4)],
+    }))
+    w4_way.far()
+    work.rows13(rest4, work.finish4(bias_rows(0)), steps({
+        0: [(w5_way.lead, 1), (w5_way.lead, 2), (w5_way.lead, 3)],
+        1: [(w5_way.follow, 1), (w5_way.follow, 2), (w5_way.follow, 3)],
+        2: [(w5_way.lead, 4)],
+        3: [(w5_way.follow, 4)],
+        4: [(w5_way.lead, 5)],
+        5: [(w5_way.lead, 6), (w5_way.follow, 5)],
+        6: [(w5_way.lead, 7), (w5_way.follow, 6)],
+    }))
+    w5_way.near()
+    work.each(work.lot(work.qbuf, w5, (near_row,)), keep5, steps({1: [(w5_way.follow, 7)]}))
+    w5_way.far()
 
     work.put_two(out)
     dbias[...] = jnp.zeros_like(dbias)
     db4, db5 = dbias.at[0, 0:8], dbias.at[0, 8:16]
-    work.rows13(work.conv(work.qbuf, w5), work.finish5(bias_rows(1), db5))
+    work.rows13(rest5, work.finish5(bias_rows(1), db5))
     work.fetch_end(cot)
     for one in gather:
         one.sent()

time: 212 us -> 210 us (level)
  Pallas kernels: 200 us -> 197 us
    pallas_call x1, Pallas kernels: 200 us -> 197 us  [cube_shards(): pl.pallas_call(functools.partial(cube_kernel, sz), out_shape=(jax.ShapeDt...]
where the time goes in v4:
time: 210 us; the launch traced here: 209 us
  Pallas kernels  197 us (94%)
  local copies, waits for them, and re-layouts  9.98 us (5%)
    pallas_call x1, Pallas kernels, cube_shards(): pl.pallas_call(functools.partial(cube_kernel, sz), out_shape=(jax.ShapeDt...  197 us
    unnamed x10, local copies, waits for them, and re-layouts  8.71 us

profile of v4, /device:TPU:0, one launch (start us, length us, event | category | flops | bytes accessed | tf_op | source)
XLA Modules:
  0.0 209.2 jit_solution(16831282180934444698)
XLA Ops:
  0.7 0.7 fusion.3
  1.3 0.7 pad_select_fusion.bias_in
  2.0 197.2 %shard_map.118 = (bf16[18,13,13,512]{3,2,1,0:T(8,128)(2,1)}, bf16[18,13,13,512]{3,2,1,0:T(8,128)(2,1)}, f32[288,1024]{1,0:T(8,128)}, f32[288,1024]{1,0:T(8,128)}, f32[2,512]{1,0:T(2,128)}) custom-call(bf16[18,13,13,512]{3,2,1,0:T(8,128)(2,1)} %images.1, bf16[18,13,13,512]{3,2,1,0:T(8,128)(2,1)} %cot.1, bf16[288,1024]{1,0:T(8,128)(2,1)} %w4_in.1, ...), custom_call_target="tpu_custom_call" | custom-call | tf_op jit(solution)/shard_map/pallas_call | solution.py:949
  199.2 0.8 constant_dynamic-slice_fusion
  200.0 0.5 slice_bitcast_fusion
  200.5 0.0 copy-start
  200.5 4.6 %copy.17 = bf16[18,13,13,512]{3,2,1,0:T(8,128)(2,1)} copy(bf16[18,13,13,512]{3,2,1,0:T(8,128)(2,1)} %get-tuple-element.24) | data formatting | bytes 6230016
  205.1 0.0 copy-done
  205.1 0.0 copy-start.2
  205.1 0.0 copy-start.1
  205.1 2.0 copy.18
  207.0 0.1 copy-done.2
  207.2 1.0 copy.19
  208.2 0.0 copy-done.1
  208.2 1.0 copy.20
Async XLA Ops:
  200.5 4.6 %copy-start = (bf16[18,13,13,512]{3,2,1,0:T(8,128)(2,1)S(1)}, bf16[18,13,13,512]{3,2,1,0:T(8,128)(2,1)}, u32[]{:S(2)}) copy-start(bf16[18,13,13,512]{3,2,1,0:T(8,128)(2,1)} %get-tuple-element.25) | copy-start | bytes 9345028
  205.1 2.1 %copy-start.2 = (f32[288,1024]{1,0:T(8,128)S(1)}, f32[288,1024]{1,0:T(8,128)}, u32[]{:S(2)}) copy-start(f32[288,1024]{1,0:T(8,128)} %get-tuple-element.26) | copy-start | bytes 3538948
  205.1 3.1 %copy-start.1 = (f32[288,1024]{1,0:T(8,128)S(1)}, f32[288,1024]{1,0:T(8,128)}, u32[]{:S(2)}) copy-start(f32[288,1024]{1,0:T(8,128)} %get-tuple-element.28) | copy-start | bytes 3538948

commit v5 on v4

--- a/solution.py
+++ b/solution.py
@@ -915,8 +915,8 @@
         work.back(work.qbuf, w4), work.finish_back4,
         steps({
             2: [(scatter4.sum_far, 1)],
-            4: [(scatter4.relay,)],
             5: [(scatter4.sum_far, 0)],
+            6: [(scatter4.relay,)],
         }),
     )
     others(lambda m: db_from(m).wait_recv())

time: 210 us -> 213 us (1.014)
  Pallas kernels: 197 us -> 200 us
    pallas_call x1, Pallas kernels: 197 us -> 200 us  [cube_shards(): pl.pallas_call(functools.partial(cube_kernel, sz), out_shape=(jax.ShapeDt...]
where the time goes in v5:
time: 213 us; the launch traced here: 212 us
  Pallas kernels  200 us (94%)
  local copies, waits for them, and re-layouts  9.98 us (5%)
    pallas_call x1, Pallas kernels, cube_shards(): pl.pallas_call(functools.partial(cube_kernel, sz), out_shape=(jax.ShapeDt...  200 us
    unnamed x10, local copies, waits for them, and re-layouts  8.71 us

profile of v5, /device:TPU:0, one launch (start us, length us, event | category | flops | bytes accessed | tf_op | source)
XLA Modules:
  0.0 212.3 jit_solution(2187461615356525372)
XLA Ops:
  0.7 0.7 fusion.3
  1.3 0.7 pad_select_fusion.bias_in
  2.0 200.3 %shard_map.118 = (bf16[18,13,13,512]{3,2,1,0:T(8,128)(2,1)}, bf16[18,13,13,512]{3,2,1,0:T(8,128)(2,1)}, f32[288,1024]{1,0:T(8,128)}, f32[288,1024]{1,0:T(8,128)}, f32[2,512]{1,0:T(2,128)}) custom-call(bf16[18,13,13,512]{3,2,1,0:T(8,128)(2,1)} %images.1, bf16[18,13,13,512]{3,2,1,0:T(8,128)(2,1)} %cot.1, bf16[288,1024]{1,0:T(8,128)(2,1)} %w4_in.1, ...), custom_call_target="tpu_custom_call" | custom-call | tf_op jit(solution)/shard_map/pallas_call | solution.py:949
  202.3 0.8 constant_dynamic-slice_fusion
  203.1 0.5 slice_bitcast_fusion
  203.6 0.0 copy-start
  203.6 4.6 %copy.17 = bf16[18,13,13,512]{3,2,1,0:T(8,128)(2,1)} copy(bf16[18,13,13,512]{3,2,1,0:T(8,128)(2,1)} %get-tuple-element.24) | data formatting | bytes 6230016
  208.2 0.0 copy-done
  208.2 0.0 copy-start.2
  208.2 0.0 copy-start.1
  208.2 2.0 copy.18
  210.1 0.1 copy-done.2
  210.3 1.0 copy.19
  211.3 0.0 copy-done.1
  211.3 1.0 copy.20
Async XLA Ops:
  203.6 4.6 %copy-start = (bf16[18,13,13,512]{3,2,1,0:T(8,128)(2,1)S(1)}, bf16[18,13,13,512]{3,2,1,0:T(8,128)(2,1)}, u32[]{:S(2)}) copy-start(bf16[18,13,13,512]{3,2,1,0:T(8,128)(2,1)} %get-tuple-element.25) | copy-start | bytes 9345028
  208.2 2.1 copy-start.2
  208.2 3.1 %copy-start.1 = (f32[288,1024]{1,0:T(8,128)S(1)}, f32[288,1024]{1,0:T(8,128)}, u32[]{:S(2)}) copy-start(f32[288,1024]{1,0:T(8,128)} %get-tuple-element.28) | copy-start | bytes 3538948
